TPU v7x, 256 devices: a whole 4x4x8 slice. The times are simulated.
256 devices in a mesh: ctx: 64 (over y, z, core), kvh: 4 (over x).
Axes of the slice: x: 4, y: 4, z: 8, core: 2. Of those that a mesh axis runs over, the one named last changes fastest.
Arguments:
- queries: bfloat16 [256, 64, 128], P('ctx', 'kvh'), may hold values from -30 to 30
- span_keys: bfloat16 [256, 8, 128], P('ctx', 'kvh'), may hold values from -16 to 16
- span_values: bfloat16 [256, 8, 128], P('ctx', 'kvh'), may hold values from -12 to 12
- cache_keys: bfloat16 [524288, 8, 128], P('ctx', 'kvh'), may hold values from -16 to 16
- cache_values: bfloat16 [524288, 8, 128], P('ctx', 'kvh'), may hold values from -7 to 7
- gating: int32 [64, 12], P('kvh'), may hold values from 0 to 127, all different within a row; in each aligned block of 16 rows (0 to 15, 16 to 31, ...) at most 3 rows name the same one
- out_weight: bfloat16 [8192, 8192], P('kvh', 'ctx'), may hold values from -0.0625 to 0.0625
Outputs:
- attended: bfloat16 [256, 64, 128], P('ctx', 'kvh')
- projected: bfloat16 [256, 8192], P('kvh', 'ctx')
Inputs may be any that keep to these rules, and one draw needn't show every extreme that they name: `gating`: each row names 12 distinct blocks. Among the heads of one index of kvh no block is named by more than 3 heads, and some block is named by exactly 3.
All inputs are finite; a program needn't handle non-finite values.
Results may differ from a plain program's by a relative error of at most 0.015.
Values may be sent and summed in bfloat16 or wider, within the bound.
A program may use at most 128 MiB of HBM per device.

v0:
```python
import jax
import jax.numpy as jnp
from jax import lax
from jax.sharding import PartitionSpec as P

BLOCK_POSITIONS = 4096


NEG = -1e30


def block_partial(query, keys, values, scale):
    scores = jnp.dot(query, keys.T, preferred_element_type=jnp.float32) * scale
    top = jnp.max(scores, axis=1)
    weights = jnp.exp(scores - top[:, None])
    total = jnp.sum(weights, axis=1)
    out = jnp.dot(weights.astype(jnp.bfloat16), values, preferred_element_type=jnp.float32)
    return (top, total, out)


def slot_table(gating, blocks, most):
    chosen = jnp.any(gating[None, :, :] == blocks[:, None, None], axis=2)
    ranks = jnp.cumsum(chosen.astype(jnp.int32), axis=1) - 1
    places = jnp.arange(most, dtype=jnp.int32)
    return chosen[:, None, :] & (ranks[:, None, :] == places[None, :, None])


def slot_maxima(onehot, maxima):
    return jnp.max(jnp.where(onehot[:, None, :], maxima[:, :, None], NEG), axis=0)


def weigh_slots(onehot, maxima, totals, outs, top):
    ones = onehot.astype(jnp.float32)
    valid = jnp.sum(ones, axis=1) > 0.5
    slot_top = jnp.einsum("kh,rh->kr", ones, top, precision=lax.Precision.HIGHEST)
    factors = jnp.where(valid[:, None], jnp.exp(maxima - slot_top), 0.0)
    numer = jnp.einsum(
        "kh,krd->rhd", ones, factors[:, :, None] * outs, precision=lax.Precision.HIGHEST
    )
    denom = jnp.einsum("kh,kr->rh", ones, factors * totals, precision=lax.Precision.HIGHEST)
    return (numer, denom)


def own_partial(queries, keys_all, values_all, first_row, scale):
    rows = queries.shape[0]
    groups = keys_all.shape[1]
    group_factor = queries.shape[1] // groups
    width = queries.shape[2]
    length = keys_all.shape[0]
    row_pos = first_row + jnp.repeat(jnp.arange(rows, dtype=jnp.int32), group_factor)
    causal = jnp.arange(length, dtype=jnp.int32)[None, :] <= row_pos[:, None]
    maxima, totals, outs = ([], [], [])
    for group in range(groups):
        query = queries[:, group * group_factor : (group + 1) * group_factor, :].reshape(
            rows * group_factor, width
        )
        scores = jnp.dot(query, keys_all[:, group, :].T, preferred_element_type=jnp.float32) * scale
        scores = jnp.where(causal, scores, NEG)
        top = jnp.max(scores, axis=1)
        weights = jnp.where(causal, jnp.exp(scores - top[:, None]), 0.0)
        maxima.append(top.reshape(rows, group_factor))
        totals.append(jnp.sum(weights, axis=1).reshape(rows, group_factor))
        outs.append(
            jnp.dot(
                weights.astype(jnp.bfloat16),
                values_all[:, group, :],
                preferred_element_type=jnp.float32,
            ).reshape(rows, group_factor, width)
        )
    return (jnp.concatenate(maxima, 1), jnp.concatenate(totals, 1), jnp.concatenate(outs, 1))


def local(queries, span_keys, span_values, cache_keys, cache_values, gating, out_weight):
    rows, heads, width = queries.shape
    groups = cache_keys.shape[1]
    group_factor = heads // groups
    topk = gating.shape[1]
    scale = width ** (-0.5)
    blocks_here = cache_keys.shape[0] // BLOCK_POSITIONS
    devices = lax.axis_size("ctx")
    position = lax.axis_index("ctx")
    total_blocks = blocks_here * devices
    most = max(3, (heads * topk + total_blocks - 1) // total_blocks + 1)
    slots = blocks_here * most
    first_row = position * rows
    head_ids = jnp.arange(heads, dtype=jnp.int32)
    keys_all, values_all = (
        lax.all_gather(span_keys, "ctx", axis=0, tiled=True),
        lax.all_gather(span_values, "ctx", axis=0, tiled=True),
    )
    own_max, own_total, own_out = own_partial(queries, keys_all, values_all, first_row, scale)
    own_blocks = position * blocks_here + jnp.arange(blocks_here, dtype=jnp.int32)
    own_table = slot_table(gating, own_blocks, most).reshape(slots, heads)
    own_heads = jnp.sum(own_table.astype(jnp.int32) * head_ids[None, :], axis=1)
    queries_all = lax.all_gather(queries, "ctx", axis=0, tiled=True)
    maxima, totals, outs = ([], [], [])
    for slot in range(slots):
        block = slot // most
        group = own_heads[slot] // group_factor
        keys = lax.dynamic_index_in_dim(
            cache_keys[block * BLOCK_POSITIONS : (block + 1) * BLOCK_POSITIONS], group, 1, False
        )
        values = lax.dynamic_index_in_dim(
            cache_values[block * BLOCK_POSITIONS : (block + 1) * BLOCK_POSITIONS], group, 1, False
        )
        keys, values = (keys, values)
        query = lax.dynamic_index_in_dim(queries_all, own_heads[slot], 1, False)
        top, total, out = block_partial(query, keys, values, scale)
        maxima.append(top)
        totals.append(total)
        outs.append(out)
    maxima = jnp.stack(maxima)
    totals = jnp.stack(totals)
    outs = jnp.stack(outs)
    top_all = lax.pmax(slot_maxima(own_table, maxima), "ctx")
    numer, denom = weigh_slots(own_table, maxima, totals, outs, top_all)
    numer, denom = (
        lax.psum_scatter(numer, "ctx", scatter_dimension=0, tiled=True),
        lax.psum_scatter(denom, "ctx", scatter_dimension=0, tiled=True),
    )
    top_rows = lax.dynamic_slice_in_dim(top_all, first_row, rows, 0)
    top = jnp.maximum(top_rows, own_max)
    carried = jnp.exp(top_rows - top)
    numer = numer * carried[:, :, None]
    denom = denom * carried
    own_factor = jnp.exp(own_max - top)
    numer = numer + own_factor[:, :, None] * own_out
    denom = denom + own_factor * own_total
    attended = (numer / denom[:, :, None]).astype(jnp.bfloat16)
    flat = attended.reshape(rows, heads * width)
    partial_rows = jnp.dot(
        lax.all_gather(flat, "ctx", axis=0, tiled=True),
        out_weight,
        preferred_element_type=jnp.float32,
    )
    projected = lax.psum_scatter(
        partial_rows.astype(jnp.bfloat16), "kvh", scatter_dimension=0, tiled=True
    )
    return (attended, projected)


def solution(mesh):
    placed = (
        P("ctx", "kvh", None),
        P("ctx", "kvh", None),
        P("ctx", "kvh", None),
        P("ctx", "kvh", None),
        P("ctx", "kvh", None),
        P("kvh", None),
        P("kvh", "ctx"),
    )
    return jax.shard_map(
        local,
        mesh=mesh,
        in_specs=placed,
        out_specs=(P("ctx", "kvh", None), P("kvh", "ctx")),
        check_vma=False,
    )
```

profile of v0, /device:TPU:1, one launch (start us, length us, event | category | flops | bytes accessed | tf_op | source)
XLA Modules:
  0.0 820.3 jit_solution(2480524258934864098)
XLA Ops:
  8.0 0.9 compare_reduce_fusion
  29.2 54.3 %all_gather.13 = bf16[256,2,128]{2,1,0:T(2,128)(2,1)S(1)} all-gather(bf16[4,2,128]{2,1,0:T(2,128)(2,1)} %param.8), channel_id=1, replica_groups=mesh['ctx'=64,'kvh'=4] {'ctx'}, dimensions={0}, use_global_device_ids=true | all-gather | bytes 133120 | tf_op jit(solution)/shard_map/all_gather | solution.py:88
  83.8 5.7 fusion.106
  94.0 16.4 %constant_dynamic-slice_fusion.7 = (bf16[4096,1,128]{2,1,0:T(2,128)(2,1)}, bf16[4096,1,128]{2,1,0:T(2,128)(2,1)}, bf16[4096,1,128]{2,1,0:T(2,128)(2,1)}, bf16[40...) fusion(bf16[4096,2,128]{2,1,0:T(2,128)(2,1)S(1)} %get-tuple-element.9, ...), kind=kLoop, calls=%fused_computation.117 | loop fusion | bytes 12582936 | tf_op jit(solution)/shard_map/jit(dynamic_index_in_dim)/dynamic_slice | solution.py:100
  110.4 3.0 fusion.105
  113.3 14.2 %constant_dynamic-slice_fusion.1 = (bf16[4096,1,128]{2,1,0:T(2,128)(2,1)S(1)}, bf16[4096,1,128]{2,1,0:T(2,128)(2,1)}, bf16[4096,1,128]{2,1,0:T(2,128)(2,1)}, bf1...) fusion(bf16[4096,2,128]{2,1,0:T(2,128)(2,1)S(1)} %get-tuple-element.7, ...), kind=kLoop, calls=%fused_computation.111 | loop fusion | bytes 12582936 | tf_op jit(solution)/shard_map/jit(dynamic_index_in_dim)/dynamic_slice | solution.py:103
  127.5 3.2 constant_dynamic-slice_fusion.8
  130.7 4.4 fusion.112
  135.1 2.7 fusion.113
  137.8 2.7 fusion.114
  140.5 2.7 fusion.115
  143.2 2.7 fusion.116
  145.8 2.7 fusion.117
  148.7 243.1 %pmax.7 = f32[256,16]{1,0:T(8,128)S(1)} all-reduce(f32[256,16]{1,0:T(8,128)S(1)} %copy.87), channel_id=1, replica_groups=mesh['ctx'=64,'kvh'=4] {'ctx'}, use_global_device_ids=true, to_apply=%region_11.12 | all-reduce | flops 4096 | bytes 32768 | tf_op jit(solution)/shard_map/pmax | solution.py:115
  391.9 3.9 fusion.33
  396.0 2.7 fusion.39
  398.8 2.7 fusion.45
  401.5 0.9 fusion.51
  402.4 0.9 fusion.57
  403.9 0.9 fusion.63
  405.2 2.7 convolution_bitcast_fusion
  409.9 52.4 %all_gather.14 = bf16[256,2,128]{2,1,0:T(2,128)(2,1)S(1)} all-gather(bf16[4,2,128]{2,1,0:T(2,128)(2,1)S(1)} %copy-done.21), channel_id=1, replica_groups=mesh['ctx'=64,'kvh'=4] {'ctx'}, dimensions={0}, use_global_device_ids=true | all-gather | bytes 133120 | tf_op jit(solution)/shard_map/all_gather | solution.py:89
  462.9 3.1 fusion
  466.0 0.7 fusion.2
  466.7 0.7 fusion.4
  467.5 0.9 copy-done.6
  472.0 243.4 %all-reduce = f32[256,16]{1,0:T(8,128)S(1)} all-reduce(f32[256,16]{1,0:T(8,128)S(1)} %fusion.92), channel_id=3, replica_groups=mesh['ctx'=64,'kvh'=4] {'ctx'}, use_global_device_ids=true, to_apply=%region_21.22.clone | all-reduce | flops 4096 | bytes 32768
  715.4 0.9 fusion.75
  717.0 75.8 %all-gather.6.cloned.1.call-done = bf16[64,4,2048]{2,1,0:T(4,128)(2,1)} async-done(((bf16[1,4,2048]{2,1,0:T(4,128)(2,1)}), bf16[64,4,2048]{2,1,0:T(4,128)(2,1)}) %all-gather.6.cloned.1.call-update) | async-done | bytes 1048592 | tf_op jit(solution)/shard_map/all_gather | solution.py:132
  792.8 1.3 reshape.121
  794.2 1.0 convolution_convert_fusion
  795.2 18.5 %reduce-scatter.5.cloned.1.call-done = bf16[64,128]{1,0:T(8,128)(2,1)} async-done(((bf16[256,128]{1,0:T(8,128)(2,1)}), bf16[64,128]{1,0:T(8,128)(2,1)}) %reduce-scatter.5.cloned.1.call-update) | async-done | bytes 16400 | tf_op jit(solution)/shard_map/reduce_scatter | solution.py:136
  (98 shorter events, 10.5 us)
Async XLA Ops:
  7.2 787.0 %copy-start = (bf16[2048,128]{1,0:T(8,128)(2,1)S(1)}, bf16[2048,128]{1,0:T(8,128)(2,1)}, u32[]{:S(2)}) copy-start(bf16[2048,128]{1,0:T(8,128)(2,1)} %param.13) | copy-start | bytes 1572868
  7.2 120.3 %all-gather.4.cloned.1.call-start = ((), (), s32[]{:S(2)}) async-start(), calls=%async_computation.2 | async-start | bytes 1064960 | tf_op jit(solution)/shard_map/all_gather | solution.py:95
  7.9 707.5 %reduce-scatter.3.cloned.1.call-start = ((), (), s32[]{:S(2)}) async-start(), calls=%async_computation.3 | async-start | bytes 2129920 | tf_op jit(solution)/shard_map/reduce_scatter | solution.py:118
  83.8 9.7 %copy-start.20 = (bf16[4,16,128]{2,1,0:T(8,128)(2,1)S(1)}, bf16[4,16,128]{2,1,0:T(8,128)(2,1)}, u32[]{:S(2)}) copy-start(bf16[4,16,128]{2,1,0:T(8,128)(2,1)} %param.7) | copy-start | bytes 49156
  94.0 16.4 %copy-start.18 = (bf16[8192,2,128]{2,1,0:T(2,128)(2,1)S(1)}, bf16[8192,2,128]{2,1,0:T(2,128)(2,1)}, u32[]{:S(2)}) copy-start(bf16[8192,2,128]{2,1,0:T(2,128)(2,1)} %param.11) | copy-start | bytes 12582916
  127.5 7.6 copy-start.17
  130.7 7.1 copy-start.16
  135.1 5.4 copy-start.15
  137.8 5.4 copy-start.14
  140.5 5.3 copy-start.13
  391.8 4.1 copy-start.1
  391.8 6.9 copy-start.3
  396.0 5.5 copy-start.5
  396.0 5.5 copy-start.12
  398.7 3.7 copy-start.7
  398.8 3.7 copy-start.11
  401.5 2.4 copy-start.9
  404.9 3.8 copy-start.22
  404.9 5.0 copy-start.21
  407.9 384.9 %all-gather.6.cloned.1.call-start = ((), (), s32[]{:S(2)}) async-start(), calls=%async_computation.5 | async-start | bytes 1064960 | tf_op jit(solution)/shard_map/all_gather | solution.py:132
  409.9 56.1 %copy-start.2 = (f32[256,4096]{1,0:T(8,128)S(1)}, f32[256,4096]{1,0:T(8,128)}, u32[]{:S(2)}) copy-start(f32[256,4096]{1,0:T(8,128)} %get-tuple-element.46) | copy-start | bytes 12582916
  462.9 3.8 copy-start.4
  466.0 2.3 copy-start.6
  466.7 2.9 copy-start.8
  468.3 2.6 copy-start.10
  716.3 97.5 %copy-start.19 = (bf16[4,16,128]{2,1,0:T(8,128)(2,1)}, bf16[4,16,128]{2,1,0:T(8,128)(2,1)S(1)}, u32[]{:S(2)}) copy-start(bf16[4,16,128]{2,1,0:T(8,128)(2,1)S(1)} %fusion.75) | copy-start | bytes 49156
  716.9 96.8 %reduce-scatter.5.cloned.1.call-start = ((), (), s32[]{:S(2)}) async-start(), calls=%async_computation.4 | async-start | bytes 81920 | tf_op jit(solution)/shard_map/reduce_scatter | solution.py:136
Sparse Core Ops, SparseCore 0:
  10.8 80.7 all-gather.3
  408.0 134.6 reduce-scatter.2
  717.0 75.7 all-gather.5
  795.9 17.8 reduce-scatter.4
where the time goes:
time: 822 us; the launch traced here: 820 us
  blocking collectives  593 us (72%)
  waiting for transfers between devices  95.1 us (12%)
  local copies, waits for them, and re-layouts  49.5 us (6%)
  between operations  37.7 us (5%)
  matrix products  35 us (4%)
  other arithmetic  9.53 us (1%)
    unnamed x1, blocking collectives  243 us
    pmax x1, blocking collectives, local(): top_all = lax.pmax(slot_maxima(own_table, maxima), 'ctx')  243 us
    all_gather x1, waiting for transfers between devices, local(): lax.all_gather(flat, 'ctx', axis=0, tiled=True)  75.8 us
    all_gather x1, blocking collectives, local(): lax.all_gather(span_keys, 'ctx', axis=0, tiled=True)  54.3 us
    all_gather x1, blocking collectives, local(): lax.all_gather(span_values, 'ctx', axis=0, tiled=True)  52.4 us
    reduce_scatter x1, waiting for transfers between devices, local(): lax.psum_scatter(partial_rows.astype(jnp.bfloat16), 'kvh', scatter_dimens...  18.5 us
    dot_general x6, matrix products, block_partial(): scores = jnp.dot(query, keys.T, preferred_element_type=jnp.float32) * scale  17.8 us
  transfers between devices with their start and end apart: 4, of which 2 were waited for; matrix products, arithmetic and copies ran while one was open for 6% of the time, Pallas kernels for 0%

commit v1 on v0

v1 whole, which is shorter than its diff:
```python
import functools

import jax
import jax.numpy as jnp
from jax import lax
from jax.experimental import pallas as pl
from jax.experimental.pallas import tpu as pltpu
from jax.sharding import PartitionSpec as P

Y, Z, X = 4, 8, 4
BLOCK_POSITIONS = 4096
MOST = 3
CHUNK = 1024
NEG = -1e30
MESH = pl.DeviceIdType.MESH
F32, BF16 = jnp.float32, jnp.bfloat16


def offsets(n):
    near = []
    for d in range(1, n // 2 + 1):
        near.append(d)
        if d != n - d:
            near.append(n - d)
    return near


ZOFF, YOFF = offsets(Z), offsets(Y)


def dot_t(a, b):
    return lax.dot_general(a, b, (((1,), (1,)), ((), ())), preferred_element_type=F32)


def dot(a, b):
    return jnp.dot(a, b, preferred_element_type=F32)


def place(y, z, c):
    return (lax.rem(y, Y) * Z + lax.rem(z, Z)) * 2 + lax.rem(c, 2)


class Gather:
    def __init__(self, buf, y, z, c, kv, zs, ys, cs, ss):
        self.buf, self.y, self.z, self.c, self.kv = buf, y, z, c, kv
        self.zs, self.ys, self.cs, self.ss = zs, ys, cs, ss

    def copy(self, index, sem, to):
        return pltpu.make_async_remote_copy(
            src_ref=self.buf.at[index], dst_ref=self.buf.at[index],
            send_sem=self.ss, recv_sem=sem, device_id=(to, self.kv), device_id_type=MESH)

    def spread(self, jz):
        y, z, c = self.y, self.z, self.c
        index = place(y, z + Z - ([0] + ZOFF)[jz], c)
        for jy, dy in enumerate(YOFF):
            self.copy(index, self.ys.at[jz, jy], place(y + dy, z, c)).start()
        self.copy(index, self.cs, place(y, z, c + 1)).start()

    def start(self):
        y, z, c = self.y, self.z, self.c
        index = place(y, z, c)
        for j, dz in enumerate(ZOFF):
            self.copy(index, self.zs.at[j], place(y, z + dz, c)).start()
        self.spread(0)

    def along_z(self, jz):
        y, z, c = self.y, self.z, self.c
        index = place(y, z + Z - ZOFF[jz - 1], c)
        self.copy(index, self.zs.at[jz - 1], place(y, z, c + 1)).wait_recv()
        self.spread(jz)

    def along_y(self, jz):
        y, z, c = self.y, self.z, self.c
        for jy, dy in enumerate(YOFF):
            index = place(y + Y - dy, z + Z - ([0] + ZOFF)[jz], c)
            self.copy(index, self.ys.at[jz, jy], place(y, z, c + 1)).wait_recv()
            self.copy(index, self.cs, place(y, z, c + 1)).start()

    def finish(self):
        other = place(self.y, self.z, self.c + 1)
        half = self.buf.at[pl.ds(0, Y * Z)]
        pltpu.make_async_remote_copy(src_ref=half, dst_ref=half, send_sem=self.ss, recv_sem=self.cs,
                                     device_id=(other, self.kv), device_id_type=MESH).wait_recv()

    def drain(self):
        other = place(self.y, self.z, self.c + 1)
        sent = self.buf.at[pl.ds(0, (Z - 1) + Z * (Y - 1) + Y * Z)]
        pltpu.make_async_remote_copy(src_ref=sent, dst_ref=sent, send_sem=self.ss, recv_sem=self.cs,
                                     device_id=(other, self.kv), device_id_type=MESH).wait_send()


def kernel(q_ref, sk_ref, sv_ref, gat_ref, kc_ref, vc_ref, w_ref, att_ref, proj_ref,
           kraw, vraw, k0, k1, v0, v1, wv, buf, buf2, f32s, kv32, d32, qaug, acc, mm, ll, ob, pf, pay, recv,
           own_o, own_l, xp, xr,
           loc, z1, y1, c1, s1, z2, y2, c2, s2, ar, asend, xs, xrs):
    n = Y * Z * 2
    me = lax.axis_index("ctx")
    kv = lax.axis_index("kvh")
    c = lax.rem(me, 2)
    z = lax.rem(lax.div(me, 2), Z)
    y = lax.div(me, 2 * Z)
    heads = gat_ref.shape[0]
    topk = gat_ref.shape[1]
    rows = q_ref.shape[0] // heads
    per = heads // 2
    width = q_ref.shape[1]
    bp = BLOCK_POSITIONS
    np_ = n * rows
    qr = rows * heads
    log2e = 1.4426950408889634
    c2s = width ** -0.5 * log2e

    kcopy = pltpu.make_async_copy(kc_ref, kraw, loc.at[0])
    vcopy = pltpu.make_async_copy(vc_ref, vraw, loc.at[1])
    wcopy = pltpu.make_async_copy(w_ref, wv, loc.at[2])
    kcopy.start()
    vcopy.start()
    wcopy.start()

    bar = pltpu.get_barrier_semaphore()

    def greet(i, _):
        pl.semaphore_signal(bar, inc=1, device_id=(lax.rem(me + i, n), kv), device_id_type=MESH)
        return 0

    lax.fori_loop(1, n, greet, 0)
    for dx in range(1, X):
        pl.semaphore_signal(bar, inc=1, device_id=(me, lax.rem(kv + dx, X)), device_id_type=MESH)
    buf[me, 0:qr, :] = q_ref[...]
    kvr = sk_ref.shape[0]
    buf[me, qr:qr + 2 * kvr, :] = jnp.concatenate([sk_ref[...], sv_ref[...]], axis=0)
    pl.semaphore_wait(bar, n - 1 + X - 1)

    g1 = Gather(buf, y, z, c, kv, z1, y1, c1, s1)
    g1.start()

    lane = lax.broadcasted_iota(jnp.int32, (heads, 2 * n), 1)
    block_of = lax.rem(lane, n) * 2 + lax.div(lane, n)
    gat = gat_ref[...]
    chosen = jnp.zeros((heads, 2 * n), jnp.int32)
    for t in range(topk):
        chosen = jnp.maximum(chosen, (gat[:, t:t + 1] == block_of).astype(jnp.int32))
    count = jnp.zeros((1, 2 * n), jnp.int32)
    hm = [jnp.full((1, 2 * n), -1, jnp.int32) for _ in range(MOST)]
    for h in range(heads):
        ch = chosen[h:h + 1, :]
        for s in range(MOST):
            hm[s] = jnp.where((ch == 1) & (count == s), h, hm[s])
        count = count + ch
    lane1 = lax.broadcasted_iota(jnp.int32, (1, 2 * n), 1)
    own_heads = [[jnp.maximum(jnp.max(jnp.where(lane1 == b * n + me, hm[s], -1)), 0) for s in range(MOST)]
                 for b in range(2)]

    def split(raw, even, odd, first, last):
        part = d32.shape[0]

        def step(i, _):
            d32[...] = raw[pl.ds(pl.multiple_of(i * part, part), part), :].astype(F32)
            to = pl.ds(pl.multiple_of(i * (part // 2), part // 2), part // 2)
            even[to, :] = d32[pl.ds(0, part // 2, stride=2), :].astype(BF16)
            odd[to, :] = d32[pl.ds(1, part // 2, stride=2), :].astype(BF16)
            return 0

        lax.fori_loop(first, last, step, 0)

    parts = kraw.shape[0] // d32.shape[0]
    kcopy.wait()
    nz = len(ZOFF)
    for j in range(1, nz + 1):
        split(kraw, k0, k1, (j - 1) * parts // nz, j * parts // nz)
        g1.along_z(j)
    vcopy.wait()
    for j in range(nz + 1):
        split(vraw, v0, v1, j * parts // (nz + 1), (j + 1) * parts // (nz + 1))
        g1.along_y(j)
    g1.finish()

    def widen(i, _):
        f32s[pl.ds(pl.multiple_of(i * qr, qr), qr), :] = buf[i, 0:qr, :].astype(F32)
        kv32[pl.ds(pl.multiple_of(i * 2 * kvr, 2 * kvr), 2 * kvr), :] = buf[i, qr:qr + 2 * kvr, :].astype(F32)
        return 0

    lax.fori_loop(0, n, widen, 0)

    for b in range(2):
        for s in range(MOST):
            h = own_heads[b][s]
            qh = f32s[pl.ds(h, np_, stride=heads), :]
            first = (h < per).astype(F32)
            at = pl.ds(s * np_, np_)
            qaug[b, at, :] = jnp.concatenate([qh * first, qh * (1.0 - first)], axis=1).astype(BF16)

    nb = bp // CHUNK
    for b in range(2):
        acc[...] = jnp.zeros_like(acc)
        ll[...] = jnp.zeros_like(ll)
        mm[...] = jnp.full_like(mm, NEG)

        def step(i, _):
            at = pl.ds(pl.multiple_of(b * bp + i * CHUNK, CHUNK), CHUNK)
            kc = jnp.concatenate([k0[at, :], k1[at, :]], axis=1)
            vc = jnp.concatenate([v0[at, :], v1[at, :]], axis=1)
            for s in range(MOST):
                sl = pl.ds(s * np_, np_)
                sc = dot_t(qaug[b, sl, :], kc)
                m0 = mm[sl, :]
                m1 = jnp.maximum(m0, jnp.max(sc, axis=1, keepdims=True) * c2s)
                p = jnp.exp2(sc * c2s - m1[:, :1])
                al = jnp.exp2(m0 - m1)
                ps = p[:, :128]
                for j in range(1, CHUNK // 128):
                    ps = ps + p[:, j * 128:(j + 1) * 128]
                ll[sl, :] = ll[sl, :] * al + ps
                mm[sl, :] = m1
                acc[sl, :] = acc[sl, :] * jnp.concatenate([al, al], axis=1) + dot(p.astype(BF16), vc)
            return 0

        lax.fori_loop(0, nb, step, 0)

        ln = lax.broadcasted_iota(jnp.int32, (np_, 128), 1)
        rw = lax.rem(lax.broadcasted_iota(jnp.int32, (np_, 128), 0), rows)
        stat = jnp.zeros((np_, 128), F32)
        for s in range(MOST):
            sl = pl.ds(s * np_, np_)
            tot = jnp.sum(ll[sl, :], axis=1, keepdims=True)
            lse = mm[sl, :] + jnp.log2(tot)
            first = own_heads[b][s] < per
            ob[s] = jnp.where(first, acc[sl, 0:128], acc[sl, 128:256]) * (1.0 / tot)
            hi = lse.astype(BF16).astype(F32)
            mid = (lse - hi).astype(BF16).astype(F32)
            lo = (lse - hi) - mid
            val = jnp.where(ln < 16, hi, jnp.where(ln < 32, mid, lo))
            stat = jnp.where((lax.rem(ln, 16) == s * rows + rw) & (ln < 48), val, stat)
        ob[MOST] = stat

        def pack(j, _):
            for s in range(MOST + 1):
                x = ob[s, pl.ds(pl.multiple_of(j * 8, 8), 8), :]
                pf[s * rows:(s + 1) * rows, :] = x[0:rows]
                pf[16 + s * rows:16 + (s + 1) * rows, :] = x[rows:2 * rows]
            pay[b, 2 * j] = pf[0:16, :].astype(BF16)
            pay[b, 2 * j + 1] = pf[16:32, :].astype(BF16)
            return 0

        lax.fori_loop(0, n // 2, pack, 0)
        recv[b, me] = pay[b, me]

        def send(i, _):
            to = lax.rem(me + i, n)
            pltpu.make_async_remote_copy(src_ref=pay.at[b, to], dst_ref=recv.at[b, me], send_sem=asend,
                                         recv_sem=ar.at[b], device_id=(to, kv), device_id_type=MESH).start()
            return 0

        lax.fori_loop(1, n, send, 0)

    kk, vvv = [], []
    for g in range(2):
        kk.append(jnp.concatenate([kv32[pl.ds(2 * i + g, n, stride=2 * kvr), :] for i in range(rows)], axis=0))
        vvv.append(jnp.concatenate([kv32[pl.ds(kvr + 2 * i + g, n, stride=2 * kvr), :] for i in range(rows)], axis=0))
    ks = jnp.concatenate(kk, axis=1).astype(BF16)
    vs = jnp.concatenate(vvv, axis=1).astype(BF16)
    qf = q_ref[...].astype(F32)
    rid = lax.broadcasted_iota(jnp.int32, (qr, 128), 0)
    first = (lax.rem(rid, heads) < per).astype(F32)
    qo = jnp.concatenate([qf * first, qf * (1.0 - first)], axis=1).astype(BF16)
    sc = dot_t(qo, ks) * c2s
    kid = lax.broadcasted_iota(jnp.int32, (qr, np_), 1)
    key_pos = lax.rem(kid, n) * rows + lax.div(kid, n)
    row_pos = me * rows + lax.div(lax.broadcasted_iota(jnp.int32, (qr, np_), 0), heads)
    seen = key_pos <= row_pos
    sc = jnp.where(seen, sc, NEG)
    om = jnp.max(sc, axis=1, keepdims=True)
    ow = jnp.where(seen, jnp.exp2(sc - om), 0.0)
    ot = jnp.sum(ow, axis=1, keepdims=True)
    oo = dot(ow.astype(BF16), vs)
    own_o[...] = jnp.where(first > 0.5, oo[:, 0:128], oo[:, 128:256]) * (1.0 / ot)
    own_l[...] = jnp.broadcast_to(om + jnp.log2(ot), (qr, 128))

    for b in range(2):
        rest = pay.at[b, pl.ds(0, n - 1)]
        pltpu.make_async_remote_copy(src_ref=rest, dst_ref=rest, send_sem=asend, recv_sem=ar.at[b],
                                     device_id=(lax.rem(me + 1, n), kv), device_id_type=MESH).wait_recv()
        f32s[b * n * 16:(b + 1) * n * 16, :] = recv[b].reshape(n * 16, 128).astype(F32)
    st = sum(f32s[pl.ds(MOST * rows + i, 2 * n, stride=16), :] for i in range(rows))
    st = (st + pltpu.roll(st, 128 - 16, 1)) + pltpu.roll(st, 128 - 32, 1)
    st = st.T
    hid = lax.broadcasted_iota(jnp.int32, (heads, 2 * n), 0)
    for i in range(rows):
        at = pl.ds(i * heads, heads)
        own = own_l[at, 0:1]
        top = own
        xs_ = []
        for s in range(MOST):
            x = jnp.where(hm[s] == hid, st[s * rows + i:s * rows + i + 1, :], NEG)
            xs_.append(x)
            top = jnp.maximum(top, jnp.max(x, axis=1, keepdims=True))
        share = jnp.exp2(own - top)
        den = share
        num = share * own_o[at, :]
        for s in range(MOST):
            wt = jnp.exp2(xs_[s] - top)
            den = den + jnp.sum(wt, axis=1, keepdims=True)
            hi = wt.astype(BF16)
            lo = (wt - hi.astype(F32)).astype(BF16)
            r = f32s[pl.ds(s * rows + i, 2 * n, stride=16), :].astype(BF16)
            both = dot(jnp.concatenate([hi, lo], axis=0), r)
            num = num + (both[0:heads] + both[heads:2 * heads])
        a = (num / den).astype(BF16)
        att_ref[at, :] = a
        buf2[me, at, :] = a

    g2 = Gather(buf2, y, z, c, kv, z2, y2, c2, s2)
    g2.start()
    for j in range(1, nz + 1):
        g2.along_z(j)
    for j in range(nz + 1):
        g2.along_y(j)
    g2.finish()

    def widen2(i, _):
        f32s[pl.ds(pl.multiple_of(i * qr, qr), qr), :] = buf2[i].astype(F32)
        return 0

    lax.fori_loop(0, n, widen2, 0)
    wcopy.wait()
    out = jnp.zeros((np_, 128), F32)
    for h in range(0, heads, 2):
        a = jnp.concatenate([f32s[pl.ds(h, np_, stride=heads), :], f32s[pl.ds(h + 1, np_, stride=heads), :]], axis=1)
        out = out + dot(a.astype(BF16), wv[h * width:(h + 2) * width, :])
    share = np_ // X
    for x in range(X):
        xp[x] = out[x * share:(x + 1) * share].astype(BF16)
    xr[kv] = xp[kv]
    for dx in range(1, X):
        to = lax.rem(kv + dx, X)
        pltpu.make_async_remote_copy(src_ref=xp.at[to], dst_ref=xr.at[kv], send_sem=xs.at[dx - 1],
                                     recv_sem=xrs.at[dx - 1], device_id=(me, to), device_id_type=MESH).start()
    for dx in range(1, X):
        to = lax.rem(kv + dx, X)
        pltpu.make_async_remote_copy(src_ref=xp.at[to], dst_ref=xr.at[lax.rem(kv + X - dx, X)], send_sem=xs.at[dx - 1],
                                     recv_sem=xrs.at[dx - 1], device_id=(me, to), device_id_type=MESH).wait()
    total = xr[0].astype(F32)
    for x in range(1, X):
        total = total + xr[x].astype(F32)
    proj_ref[...] = total.astype(BF16)

    g1.drain()
    g2.drain()
    for b in range(2):
        rest = pay.at[b, pl.ds(0, n - 1)]
        pltpu.make_async_remote_copy(src_ref=rest, dst_ref=rest, send_sem=asend, recv_sem=ar.at[b],
                                     device_id=(lax.rem(me + 1, n), kv), device_id_type=MESH).wait_send()


def local(queries, span_keys, span_values, cache_keys, cache_values, gating, out_weight):
    rows, heads, width = queries.shape
    groups = span_keys.shape[1]
    n = Y * Z * 2
    np_ = n * rows
    qr = rows * heads
    kvr = rows * groups
    bp = BLOCK_POSITIONS
    raw = 2 * bp * groups
    part = min(1024, raw)
    nzo, nyo = len(ZOFF), len(YOFF)
    vm = pltpu.VMEM
    dma = pltpu.SemaphoreType.DMA
    scratch = [
        vm((raw, width), BF16), vm((raw, width), BF16),
        vm((2 * bp, width), BF16), vm((2 * bp, width), BF16), vm((2 * bp, width), BF16), vm((2 * bp, width), BF16),
        vm(out_weight.shape, BF16),
        vm((n, qr + 2 * kvr, width), BF16), vm((n, qr, width), BF16),
        vm((n * qr, width), F32), vm((n * 2 * kvr, width), F32), vm((part, width), F32),
        vm((2, MOST * np_, 2 * width), BF16),
        vm((MOST * np_, 2 * width), F32), vm((MOST * np_, width), F32), vm((MOST * np_, width), F32),
        vm((MOST + 1, np_, width), F32), vm((32, width), F32),
        vm((2, n, 16, width), BF16), vm((2, n, 16, width), BF16),
        vm((qr, width), F32), vm((qr, width), F32),
        vm((X, np_ // X, width), BF16), vm((X, np_ // X, width), BF16),
        dma((3,)),
        dma((nzo,)), dma((nzo + 1, nyo)), dma, dma,
        dma((nzo,)), dma((nzo + 1, nyo)), dma, dma,
        dma((2,)), dma, dma((X - 1,)), dma((X - 1,)),
    ]
    inv = pl.BlockSpec(memory_space=pltpu.VMEM)
    anyw = pl.BlockSpec(memory_space=pl.ANY)
    att, proj = pl.pallas_call(
        kernel,
        out_shape=(jax.ShapeDtypeStruct((qr, width), BF16), jax.ShapeDtypeStruct((np_ // X, width), BF16)),
        in_specs=[inv, inv, inv, inv, anyw, anyw, anyw],
        out_specs=(inv, inv),
        scratch_shapes=scratch,
        compiler_params=pltpu.CompilerParams(collective_id=0, has_side_effects=True, vmem_limit_bytes=60 << 20),
        name="sparse_attention",
    )(
        queries.reshape(qr, width), span_keys.reshape(kvr, width), span_values.reshape(kvr, width), gating,
        cache_keys.reshape(raw, width), cache_values.reshape(raw, width), out_weight,
    )
    return att.reshape(rows, heads, width), proj


def solution(mesh):
    placed = (
        P("ctx", "kvh", None),
        P("ctx", "kvh", None),
        P("ctx", "kvh", None),
        P("ctx", "kvh", None),
        P("ctx", "kvh", None),
        P("kvh", None),
        P("kvh", "ctx"),
    )
    return jax.shard_map(
        local,
        mesh=mesh,
        in_specs=placed,
        out_specs=(P("ctx", "kvh", None), P("kvh", "ctx")),
        check_vma=False,
    )
```

time: 822 us -> 73 us (0.09)
  blocking collectives: 593 us -> 0 us
  waiting for transfers between devices: 95.1 us -> 0 us
  Pallas kernels: 0 us -> 69.3 us
  local copies, waits for them, and re-layouts: 49.5 us -> 2.65 us
  between operations: 37.7 us -> 0.64 us
  matrix products: 35 us -> 0 us
  other arithmetic: 9.53 us -> 0 us
    unnamed x1 -> x0, blocking collectives: 243 us -> none
    pmax x1 -> x0, blocking collectives: 243 us -> none  [local(): top_all = lax.pmax(slot_maxima(own_table, maxima), 'ctx')]
    all_gather x2 -> x0, blocking collectives: 107 us -> none  [the longest x1 54.3 us: local(): lax.all_gather(span_keys, 'ctx', axis=0, tiled=True)]
    all_gather x2 -> x0, waiting for transfers between devices: 75.8 us -> none  [the longest x1 75.8 us: local(): lax.all_gather(flat, 'ctx', axis=0, tiled=True)]
    pallas_call x0 -> x1, Pallas kernels: none -> 69.3 us  [local(): pl.pallas_call(kernel, out_shape=(jax.ShapeDtypeStruct((qr, width), BF16)...]
    dot_general x20 -> x0, matrix products: 35 us -> none  [the longest x6 17.8 us: block_partial(): scores = jnp.dot(query, keys.T, preferred_element_type=jnp.float32) * scale]
    dynamic_slice x3 -> x0, local copies, waits for them, and re-layouts: 33.7 us -> none  [the longest x1 16.4 us: local(): lax.dynamic_index_in_dim(cache_keys[block * BLOCK_POSITIONS:(block + 1) *...]
    reduce_scatter x2 -> x0, waiting for transfers between devices: 18.5 us -> none  [the longest x1 18.5 us: local(): lax.psum_scatter(partial_rows.astype(jnp.bfloat16), 'kvh', scatter_dimens...]
  transfers between devices with their start and end apart: 4 -> 0, of which waited for: 2 -> 0; matrix products, arithmetic and copies ran while one was open for 6% -> 0% of each run, Pallas kernels for 0% -> 0%
where the time goes in v1:
time: 73 us; the launch traced here: 72.6 us
  Pallas kernels  69.3 us (95%)
  local copies, waits for them, and re-layouts  2.65 us (4%)
    pallas_call x1, Pallas kernels, local(): pl.pallas_call(kernel, out_shape=(jax.ShapeDtypeStruct((qr, width), BF16)...  69.3 us
    unnamed x2, local copies, waits for them, and re-layouts  2.65 us

profile of v1, /device:TPU:1, one launch (start us, length us, event | category | flops | bytes accessed | tf_op | source)
XLA Modules:
  0.0 72.6 jit_solution(5348199707559686551)
XLA Ops:
  0.6 69.3 %sparse_attention.1 = (bf16[64,128]{1,0:T(8,128)(2,1)}, bf16[64,128]{1,0:T(8,128)(2,1)}) custom-call(bf16[64,128]{1,0:T(8,128)(2,1)} %bitcast.8, bf16[8,128]{1,0:T(8,128)(2,1)} %bitcast.10, bf16[8,128]{1,0:T(8,128)(2,1)} %bitcast.11, s32[16,12]{1,0:T(8,128)} %gat_ref.1, bf16[16384,128]{1,0:T(8,128)(2,1)} %bitcast.6, bf16[16384,128]{1,0:T(8,128)(2,1)} %bitcast.7, ...), custom_call_target="tpu_custom_call" | custom-call | tf_op jit(solution)/shard_map/sparse_attention/pallas_call | solution.py:388
  70.0 1.3 %copy.11 = bf16[4,16,128]{2,1,0:T(8,128)(2,1)} copy(bf16[4,16,128]{2,1,0:T(8,128)(2,1)} %bitcast.9) | data formatting | bytes 32768
  71.3 1.3 %copy.12 = bf16[64,128]{1,0:T(8,128)(2,1)} copy(bf16[64,128]{1,0:T(8,128)(2,1)} %get-tuple-element.9) | data formatting | bytes 32768

commit v2 on v1

v2 whole, which is shorter than its diff:
```python
import functools

import jax
import jax.numpy as jnp
from jax import lax
from jax.experimental import pallas as pl
from jax.experimental.pallas import tpu as pltpu
from jax.sharding import PartitionSpec as P

Y, Z, X = 4, 8, 4
BLOCK_POSITIONS = 4096
MOST = 3
CHUNK = 1024
NEG = -1e30
MESH = pl.DeviceIdType.MESH
F32, BF16 = jnp.float32, jnp.bfloat16


def far_first(n):
    return sorted(range(n), key=lambda d: -min(d, n - d))


def near_first(n):
    return far_first(n)[:-1][::-1]


def dot_t(a, b):
    return lax.dot_general(a, b, (((1,), (1,)), ((), ())), preferred_element_type=F32)


def dot(a, b):
    return jnp.dot(a, b, preferred_element_type=F32)


class Comm:
    def __init__(self):
        self.me = lax.axis_index("ctx")
        self.kv = lax.axis_index("kvh")
        self.c = lax.rem(self.me, 2)
        self.z = lax.rem(lax.div(self.me, 2), Z)
        self.y = lax.div(self.me, 2 * Z)
        self.zc = 2 * self.z + self.c

    def rank(self, dy, dz, dc):
        return (lax.rem(self.y + dy, Y) * Z + lax.rem(self.z + dz, Z)) * 2 + lax.rem(self.c + dc, 2)

    def y_of(self, dy):
        return lax.rem(self.y + dy, Y)

    def zc_of(self, dz):
        return 2 * lax.rem(self.z + dz, Z) + self.c

    def copy(self, ref, send, recv, dy, dz, dc):
        return pltpu.make_async_remote_copy(src_ref=ref, dst_ref=ref, send_sem=send, recv_sem=recv,
                                            device_id=(self.rank(dy, dz, dc), self.kv), device_id_type=MESH)


class GatherZ:
    def __init__(self, m, buf, at, zs, ys, cs, sends):
        self.m, self.buf, self.at = m, buf, at
        self.zs, self.ys, self.cs, self.sends = zs, ys, cs, sends

    def spread(self, dz):
        m = self.m
        ref = self.buf.at[m.y, m.zc_of(Z - dz), self.at]
        for dy in far_first(Y)[:-1]:
            m.copy(ref, self.sends.at[1], self.ys.at[dz, dy - 1], dy, 0, 0).start()

    def start(self):
        m = self.m
        ref = self.buf.at[m.y, m.zc, self.at]
        for dz in far_first(Z)[:-1]:
            m.copy(ref, self.sends.at[0], self.zs.at[dz - 1], 0, dz, 0).start()
        self.spread(0)

    def along_z(self, dz):
        m = self.m
        m.copy(self.buf.at[m.y, m.zc_of(Z - dz), self.at], self.sends.at[0], self.zs.at[dz - 1], 0, dz, 0).wait_recv()
        self.spread(dz)

    def along_y(self, dz):
        m = self.m
        zc = m.zc_of(Z - dz)
        for dy in near_first(Y):
            m.copy(self.buf.at[m.y_of(Y - dy), zc, self.at], self.sends.at[1], self.ys.at[dz, dy - 1], dy, 0, 0).wait_recv()
        m.copy(self.buf.at[:, zc, self.at], self.sends.at[2], self.cs, 0, 0, 1).start()

    def finish(self):
        self.m.copy(self.buf.at[:, pl.ds(0, Z), self.at], self.sends.at[2], self.cs, 0, 0, 1).wait_recv()

    def drain(self):
        m = self.m
        m.copy(self.buf.at[0, pl.ds(0, Z - 1), self.at], self.sends.at[0], self.cs, 0, 0, 1).wait_send()
        m.copy(self.buf.at[pl.ds(0, Y - 1), pl.ds(0, Z), self.at], self.sends.at[1], self.cs, 0, 0, 1).wait_send()
        m.copy(self.buf.at[:, pl.ds(0, Z), self.at], self.sends.at[2], self.cs, 0, 0, 1).wait_send()


class GatherY:
    def __init__(self, m, buf, at, ys, zs, cs, sends):
        self.m, self.buf, self.at = m, buf, at
        self.ys, self.zs, self.cs, self.sends = ys, zs, cs, sends

    def start(self):
        m = self.m
        ref = self.buf.at[m.y, m.zc, self.at]
        for dy in far_first(Y)[:-1]:
            m.copy(ref, self.sends.at[0], self.ys.at[dy - 1], dy, 0, 0).start()

    def forward(self):
        m = self.m
        for dy in near_first(Y):
            m.copy(self.buf.at[m.y_of(Y - dy), m.zc, self.at], self.sends.at[0], self.ys.at[dy - 1], dy, 0, 0).wait_recv()
        ref = self.buf.at[:, m.zc, self.at]
        for dz in far_first(Z)[:-1]:
            m.copy(ref, self.sends.at[1], self.zs.at[dz - 1], 0, dz, 0).start()
        m.copy(ref, self.sends.at[2], self.cs, 0, 0, 1).start()

    def across(self, dz):
        m = self.m
        ref = self.buf.at[:, m.zc_of(Z - dz), self.at]
        m.copy(ref, self.sends.at[1], self.zs.at[dz - 1], 0, dz, 0).wait_recv()
        m.copy(ref, self.sends.at[2], self.cs, 0, 0, 1).start()

    def finish(self):
        self.m.copy(self.buf.at[:, pl.ds(0, Z), self.at], self.sends.at[2], self.cs, 0, 0, 1).wait_recv()

    def drain(self):
        m = self.m
        m.copy(self.buf.at[0, pl.ds(0, Y - 1), self.at], self.sends.at[0], self.cs, 0, 0, 1).wait_send()
        m.copy(self.buf.at[:, pl.ds(0, Z - 1), self.at], self.sends.at[1], self.cs, 0, 0, 1).wait_send()
        m.copy(self.buf.at[:, pl.ds(0, Z), self.at], self.sends.at[2], self.cs, 0, 0, 1).wait_send()


class Gather:
    def __init__(self, m, buf, sems):
        rows = buf.shape[2]
        cut = rows - rows // 4
        self.a = GatherZ(m, buf, pl.ds(0, cut), *sems[:4])
        self.b = GatherY(m, buf, pl.ds(cut, rows - cut), *sems[4:])

    def run(self, beside):
        a, b = self.a, self.b
        b.start()
        a.start()
        near = near_first(Z)
        for i, dz in enumerate(near):
            beside()
            a.along_z(dz)
            if i == min(1, len(near) - 1):
                b.forward()
        beside()
        a.along_y(0)
        for dz in near:
            beside()
            a.along_y(dz)
            b.across(dz)
        a.finish()
        b.finish()

    def drain(self):
        self.a.drain()
        self.b.drain()


def kernel(q_ref, sk_ref, sv_ref, gat_ref, kc_ref, vc_ref, w_ref, att_ref, part_ref,
           kraw, vraw, k0, k1, v0, v1, wv, buf, buf2, bufkv, f32s, kv32, d32, qaug,
           sb, cm, pb, alb, acc, mm, ll, ob, pf, pay, recv, own_o, own_l, xp,
           loc, ar, asend, xs, xrs, *sems):
    m = Comm()
    n = Y * Z * 2
    me, kv = m.me, m.kv
    heads, topk = gat_ref.shape
    rows = q_ref.shape[0] // heads
    per = heads // 2
    width = q_ref.shape[1]
    bp = BLOCK_POSITIONS
    np_ = n * rows
    qr = rows * heads
    kvr = sk_ref.shape[0]
    row = 2 * Z * rows
    hp = Y // 2 * row
    c2s = width ** -0.5 * 1.4426950408889634

    kcopy = pltpu.make_async_copy(kc_ref, kraw, loc.at[0])
    vcopy = pltpu.make_async_copy(vc_ref, vraw, loc.at[1])
    wcopy = pltpu.make_async_copy(w_ref, wv, loc.at[2])
    bar = pltpu.get_barrier_semaphore()
    for dz in far_first(Z)[:-1]:
        pl.semaphore_signal(bar, inc=1, device_id=(m.rank(0, dz, 0), kv), device_id_type=MESH)
    for dy in far_first(Y)[:-1]:
        pl.semaphore_signal(bar, inc=1, device_id=(m.rank(dy, 0, 0), kv), device_id_type=MESH)
    pl.semaphore_signal(bar, inc=1, device_id=(m.rank(0, 0, 1), kv), device_id_type=MESH)
    for dx in range(1, X):
        pl.semaphore_signal(bar, inc=1, device_id=(me, lax.rem(kv + dx, X)), device_id_type=MESH)
    kcopy.start()
    vcopy.start()
    wcopy.start()
    buf[m.y, m.zc] = q_ref[...]
    bufkv[m.y, m.zc] = jnp.concatenate([sk_ref[...], sv_ref[...]], axis=0)

    lane = lax.broadcasted_iota(jnp.int32, (heads, 2 * n), 1)
    block_of = lax.rem(lane, n) * 2 + lax.div(lane, n)
    gat = gat_ref[...]
    chosen = jnp.zeros((heads, 2 * n), jnp.int32)
    for t in range(topk):
        chosen = jnp.maximum(chosen, (gat[:, t:t + 1] == block_of).astype(jnp.int32))
    count = jnp.zeros((1, 2 * n), jnp.int32)
    hm = [jnp.full((1, 2 * n), -1, jnp.int32) for _ in range(MOST)]
    for h in range(heads):
        ch = chosen[h:h + 1, :]
        for s in range(MOST):
            hm[s] = jnp.where((ch == 1) & (count == s), h, hm[s])
        count = count + ch
    lane1 = lax.broadcasted_iota(jnp.int32, (1, 2 * n), 1)
    own_heads = [[jnp.maximum(jnp.max(jnp.where(lane1 == b * n + me, hm[s], -1)), 0) for s in range(MOST)]
                 for b in range(2)]

    part = d32.shape[0]
    parts = kraw.shape[0] // part

    def split(raw, even, odd, i):
        at = pl.ds(i * part, part)
        to = pl.ds(i * (part // 2), part // 2)
        d32[...] = raw[at, :].astype(F32)
        even[to, :] = d32[pl.ds(0, part // 2, stride=2), :].astype(BF16)
        odd[to, :] = d32[pl.ds(1, part // 2, stride=2), :].astype(BF16)

    def pieces():
        kcopy.wait()
        for i in range(parts):
            split(kraw, k0, k1, i)
            yield
        vcopy.wait()
        for i in range(parts):
            split(vraw, v0, v1, i)
            yield

    work = pieces()
    todo = 2 * parts
    each = -(-todo // (2 * Z + 1))

    def beside():
        for _ in range(each):
            next(work, None)

    beside()
    pl.semaphore_wait(bar, Z - 1 + Y - 1 + 1 + X - 1)
    g1 = Gather(m, buf, sems[0:8])
    g1.run(beside)
    for _ in work:
        pass
    g3 = GatherZ(m, bufkv, pl.ds(0, 2 * kvr), *sems[16:20])
    g3.start()

    def widen(i, _):
        zc = lax.rem(i, 2 * Z)
        f32s[pl.ds(pl.multiple_of(i * qr, qr), qr), :] = buf[lax.div(i, 2 * Z), zc].astype(F32)
        return 0

    lax.fori_loop(0, n, widen, 0)

    nb = bp // CHUNK
    far = far_first(Y)
    for half in range(2):
        dys = far[half * (Y // 2):(half + 1) * (Y // 2)]
        for b in range(2):
            for s in range(MOST):
                h = own_heads[b][s]
                first = (h < per).astype(F32)
                for t, dy in enumerate(dys):
                    qh = f32s[pl.ds(m.y_of(dy) * (row * heads) + h, row, stride=heads), :]
                    qaug[b, s * hp + t * row:s * hp + (t + 1) * row, :] = jnp.concatenate(
                        [qh * first, qh * (1.0 - first)], axis=1).astype(BF16)

        def unit(b, _):
            def both(even, odd, i):
                at = pl.ds(pl.multiple_of(b * bp + i * CHUNK, CHUNK), CHUNK)
                return jnp.concatenate([even[at, :], odd[at, :]], axis=1)

            def score(slot, i):
                s = dot_t(qaug[b], both(k0, k1, i))
                sb[slot] = s
                top = s[:, :128]
                for j in range(1, CHUNK // 128):
                    top = jnp.maximum(top, s[:, j * 128:(j + 1) * 128])
                cm[slot] = top

            def soften(slot):
                m0 = mm[...]
                m1 = jnp.maximum(m0, jnp.max(cm[slot], axis=1, keepdims=True) * c2s)
                p = jnp.exp2(sb[slot] * c2s - m1[:, :1])
                al = jnp.exp2(m0 - m1)
                ps = p[:, :128]
                for j in range(1, CHUNK // 128):
                    ps = ps + p[:, j * 128:(j + 1) * 128]
                ll[...] = ll[...] * al + ps
                mm[...] = m1
                alb[slot] = al
                pb[slot] = p.astype(BF16)

            def gain(slot, i):
                al = alb[slot]
                acc[...] = acc[...] * jnp.concatenate([al, al], axis=1) + dot(pb[slot], both(v0, v1, i))

            acc[...] = jnp.zeros_like(acc)
            ll[...] = jnp.zeros_like(ll)
            mm[...] = jnp.full_like(mm, NEG)
            score(0, 0)
            score(1, 1)
            soften(0)
            for i in range(1, nb - 1):
                score((i + 1) % 2, i + 1)
                gain((i - 1) % 2, i - 1)
                soften(i % 2)
            gain(nb % 2, nb - 2)
            soften((nb - 1) % 2)
            gain((nb - 1) % 2, nb - 1)

            ln = lax.broadcasted_iota(jnp.int32, (hp, 128), 1)
            rw = lax.rem(lax.broadcasted_iota(jnp.int32, (hp, 128), 0), rows)
            stat = jnp.zeros((hp, 128), F32)
            for s in range(MOST):
                sl = pl.ds(s * hp, hp)
                tot = jnp.sum(ll[sl, :], axis=1, keepdims=True)
                lse = mm[sl, :] + jnp.log2(tot)
                first = jnp.where(b == 0, own_heads[0][s], own_heads[1][s]) < per
                ob[s] = jnp.where(first, acc[sl, 0:128], acc[sl, 128:256]) * (1.0 / tot)
                hi = lse.astype(BF16).astype(F32)
                mid = (lse - hi).astype(BF16).astype(F32)
                lo = (lse - hi) - mid
                val = jnp.where(ln < 16, hi, jnp.where(ln < 32, mid, lo))
                stat = jnp.where((lax.rem(ln, 16) == s * rows + rw) & (ln < 48), val, stat)
            ob[MOST] = stat
            for t, dy in enumerate(dys):
                to_y = m.y_of(dy) * (2 * Z)

                def pack(j, _):
                    for s in range(MOST + 1):
                        x = ob[s, pl.ds(pl.multiple_of(t * row + j * 8, 8), 8), :]
                        pf[s * rows:(s + 1) * rows, :] = x[0:rows]
                        pf[16 + s * rows:16 + (s + 1) * rows, :] = x[rows:2 * rows]
                    pay[b, to_y + 2 * j] = pf[0:16, :].astype(BF16)
                    pay[b, to_y + 2 * j + 1] = pf[16:32, :].astype(BF16)
                    return 0

                lax.fori_loop(0, Z, pack, 0)
            if 0 in dys:
                recv[b, me] = pay[b, me]

            def send(dy, dz, dc):
                to = m.rank(dy, dz, dc)
                pltpu.make_async_remote_copy(src_ref=pay.at[b, to], dst_ref=recv.at[b, me], send_sem=asend,
                                             recv_sem=ar.at[b], device_id=(to, kv), device_id_type=MESH).start()

            def sends(i, _):
                k = lax.div(i + 1, 2)
                dz = Z // 2 + jnp.where(lax.rem(i, 2) == 1, -k, k)
                for dy in dys:
                    for dc in range(2):
                        send(dy, dz, dc)
                return 0

            lax.fori_loop(0, Z - 1, sends, 0)
            for dy in dys:
                for dc in range(2):
                    if (dy, dc) != (0, 0):
                        send(dy, 0, dc)
            return 0

        lax.fori_loop(0, 2, unit, 0)
        if half == 0:
            for dz in near_first(Z):
                g3.along_z(dz)
    for dz in range(Z):
        g3.along_y(dz)
    g3.finish()

    def widenkv(i, _):
        zc = lax.rem(i, 2 * Z)
        kv32[pl.ds(pl.multiple_of(i * 2 * kvr, 2 * kvr), 2 * kvr), :] = bufkv[lax.div(i, 2 * Z), zc].astype(F32)
        return 0

    lax.fori_loop(0, n, widenkv, 0)
    kk, vvv = [], []
    for g in range(2):
        kk.append(jnp.concatenate([kv32[pl.ds(2 * i + g, n, stride=2 * kvr), :] for i in range(rows)], axis=0))
        vvv.append(jnp.concatenate([kv32[pl.ds(kvr + 2 * i + g, n, stride=2 * kvr), :] for i in range(rows)], axis=0))
    ks = jnp.concatenate(kk, axis=1).astype(BF16)
    vs = jnp.concatenate(vvv, axis=1).astype(BF16)
    qf = q_ref[...].astype(F32)
    rid = lax.broadcasted_iota(jnp.int32, (qr, 128), 0)
    first = (lax.rem(rid, heads) < per).astype(F32)
    qo = jnp.concatenate([qf * first, qf * (1.0 - first)], axis=1).astype(BF16)
    sc = dot_t(qo, ks) * c2s
    kid = lax.broadcasted_iota(jnp.int32, (qr, np_), 1)
    key_pos = lax.rem(kid, n) * rows + lax.div(kid, n)
    row_pos = me * rows + lax.div(lax.broadcasted_iota(jnp.int32, (qr, np_), 0), heads)
    seen = key_pos <= row_pos
    sc = jnp.where(seen, sc, NEG)
    om = jnp.max(sc, axis=1, keepdims=True)
    ow = jnp.where(seen, jnp.exp2(sc - om), 0.0)
    ot = jnp.sum(ow, axis=1, keepdims=True)
    oo = dot(ow.astype(BF16), vs)
    own_o[...] = jnp.where(first > 0.5, oo[:, 0:128], oo[:, 128:256]) * (1.0 / ot)
    own_l[...] = jnp.broadcast_to(om + jnp.log2(ot), (qr, 128))

    for b in range(2):
        rest = pay.at[b, pl.ds(0, n - 1)]
        pltpu.make_async_remote_copy(src_ref=rest, dst_ref=rest, send_sem=asend, recv_sem=ar.at[b],
                                     device_id=(m.rank(0, 1, 0), kv), device_id_type=MESH).wait_recv()
        f32s[b * n * 16:(b + 1) * n * 16, :] = recv[b].reshape(n * 16, 128).astype(F32)
    st = sum(f32s[pl.ds(MOST * rows + i, 2 * n, stride=16), :] for i in range(rows))
    st = (st + pltpu.roll(st, 128 - 16, 1)) + pltpu.roll(st, 128 - 32, 1)
    st = st.T
    hid = lax.broadcasted_iota(jnp.int32, (heads, 2 * n), 0)
    for i in range(rows):
        at = pl.ds(i * heads, heads)
        own = own_l[at, 0:1]
        top = own
        xs_ = []
        for s in range(MOST):
            x = jnp.where(hm[s] == hid, st[s * rows + i:s * rows + i + 1, :], NEG)
            xs_.append(x)
            top = jnp.maximum(top, jnp.max(x, axis=1, keepdims=True))
        share = jnp.exp2(own - top)
        den = share
        num = share * own_o[at, :]
        for s in range(MOST):
            wt = jnp.exp2(xs_[s] - top)
            den = den + jnp.sum(wt, axis=1, keepdims=True)
            hi = wt.astype(BF16)
            lo = (wt - hi.astype(F32)).astype(BF16)
            r = f32s[pl.ds(s * rows + i, 2 * n, stride=16), :].astype(BF16)
            two = dot(jnp.concatenate([hi, lo], axis=0), r)
            num = num + (two[0:heads] + two[heads:2 * heads])
        a = (num / den).astype(BF16)
        att_ref[at, :] = a
        buf2[m.y, m.zc, at, :] = a

    g2 = Gather(m, buf2, sems[8:16])
    g2.run(lambda: None)
    wcopy.wait()
    share = np_ // X
    per_x = n // X
    for dxs in (far_first(X)[:X // 2], far_first(X)[X // 2:]):
        for t, dx in enumerate(dxs):
            x = lax.rem(kv + dx, X)

            def widen2(i, _):
                j = x * per_x + i
                to = pl.ds(pl.multiple_of((t * per_x + i) * qr, qr), qr)
                f32s[to, :] = buf2[lax.div(j, 2 * Z), lax.rem(j, 2 * Z)].astype(F32)
                return 0

            lax.fori_loop(0, per_x, widen2, 0)
        out = jnp.zeros((len(dxs) * share, 128), F32)
        for h in range(0, heads, 2):
            a = jnp.concatenate([f32s[pl.ds(h + e, len(dxs) * share, stride=heads), :] for e in range(2)], axis=1)
            out = out + dot(a.astype(BF16), wv[h * width:(h + 2) * width, :])
        for t, dx in enumerate(dxs):
            x = lax.rem(kv + dx, X)
            piece = out[t * share:(t + 1) * share].astype(BF16)
            if dx == 0:
                part_ref[kv] = piece
            else:
                xp[dx - 1] = piece
                pltpu.make_async_remote_copy(src_ref=xp.at[dx - 1], dst_ref=part_ref.at[kv], send_sem=xs.at[dx - 1],
                                             recv_sem=xrs.at[dx - 1], device_id=(me, x), device_id_type=MESH).start()
    g1.drain()
    g2.drain()
    g3.drain()
    for b in range(2):
        rest = pay.at[b, pl.ds(0, n - 1)]
        pltpu.make_async_remote_copy(src_ref=rest, dst_ref=rest, send_sem=asend, recv_sem=ar.at[b],
                                     device_id=(m.rank(0, 1, 0), kv), device_id_type=MESH).wait_send()
    for dx in range(1, X):
        pltpu.make_async_remote_copy(src_ref=xp.at[dx - 1], dst_ref=part_ref.at[lax.rem(kv + X - dx, X)],
                                     send_sem=xs.at[dx - 1], recv_sem=xrs.at[dx - 1],
                                     device_id=(me, lax.rem(kv + dx, X)), device_id_type=MESH).wait()


def close(att_ref, part_ref, a_ref, p_ref):
    a_ref[...] = att_ref[...]
    total = part_ref[0].astype(F32)
    for x in range(1, X):
        total = total + part_ref[x].astype(F32)
    p_ref[...] = total.astype(BF16)


def local(queries, span_keys, span_values, cache_keys, cache_values, gating, out_weight):
    rows, heads, width = queries.shape
    groups = span_keys.shape[1]
    n = Y * Z * 2
    np_ = n * rows
    qr = rows * heads
    kvr = rows * groups
    bp = BLOCK_POSITIONS
    raw = 2 * bp * groups
    part = min(1024, raw)
    unit = MOST * np_ // 2
    vm = pltpu.VMEM
    dma = pltpu.SemaphoreType.DMA
    along = [dma((Z - 1,)), dma((Z, Y - 1)), dma, dma((3,))]
    both = along + [dma((Y - 1,)), dma((Z - 1,)), dma, dma((3,))]
    scratch = [
        vm((raw, width), BF16), vm((raw, width), BF16),
        vm((2 * bp, width), BF16), vm((2 * bp, width), BF16), vm((2 * bp, width), BF16), vm((2 * bp, width), BF16),
        vm(out_weight.shape, BF16),
        vm((Y, 2 * Z, qr, width), BF16), vm((Y, 2 * Z, qr, width), BF16), vm((Y, 2 * Z, 2 * kvr, width), BF16),
        vm((n * qr, width), F32), vm((n * 2 * kvr, width), F32), vm((part, width), F32),
        vm((2, unit, 2 * width), BF16),
        vm((2, unit, CHUNK), F32), vm((2, unit, width), F32), vm((2, unit, CHUNK), BF16), vm((2, unit, width), F32),
        vm((unit, 2 * width), F32), vm((unit, width), F32), vm((unit, width), F32),
        vm((MOST + 1, np_ // 2, width), F32), vm((32, width), F32),
        vm((2, n, 16, width), BF16), vm((2, n, 16, width), BF16),
        vm((qr, width), F32), vm((qr, width), F32),
        vm((X - 1, np_ // X, width), BF16),
        dma((3,)), dma((2,)), dma, dma((X - 1,)), dma((X - 1,)),
        *both, *both, *along,
    ]
    inv = pl.BlockSpec(memory_space=pltpu.VMEM)
    anyw = pl.BlockSpec(memory_space=pl.ANY)
    att, parts = pl.pallas_call(
        kernel,
        out_shape=(jax.ShapeDtypeStruct((qr, width), BF16), jax.ShapeDtypeStruct((X, np_ // X, width), BF16)),
        in_specs=[inv, inv, inv, inv, anyw, anyw, anyw],
        out_specs=(inv, inv),
        scratch_shapes=scratch,
        compiler_params=pltpu.CompilerParams(collective_id=0, has_side_effects=True, vmem_limit_bytes=60 << 20),
        name="sparse_attention",
    )(
        queries.reshape(qr, width), span_keys.reshape(kvr, width), span_values.reshape(kvr, width), gating,
        cache_keys.reshape(raw, width), cache_values.reshape(raw, width), out_weight,
    )
    att, proj = pl.pallas_call(
        close,
        out_shape=(jax.ShapeDtypeStruct((qr, width), BF16), jax.ShapeDtypeStruct((np_ // X, width), BF16)),
        in_specs=[inv, inv],
        out_specs=(inv, inv),
        name="close",
    )(att, parts)
    return att.reshape(rows, heads, width), proj


def solution(mesh):
    placed = (
        P("ctx", "kvh", None),
        P("ctx", "kvh", None),
        P("ctx", "kvh", None),
        P("ctx", "kvh", None),
        P("ctx", "kvh", None),
        P("kvh", None),
        P("kvh", "ctx"),
    )
    return jax.shard_map(
        local,
        mesh=mesh,
        in_specs=placed,
        out_specs=(P("ctx", "kvh", None), P("kvh", "ctx")),
        check_vma=False,
    )
```

time: 73 us -> 60.4 us (0.83)
  Pallas kernels: 69.3 us -> 59.5 us
  local copies, waits for them, and re-layouts: 2.65 us -> 0 us
    pallas_call x1, Pallas kernels: 69.3 us -> 58 us  [local(): pl.pallas_call(kernel, out_shape=(jax.ShapeDtypeStruct((qr, width), BF16)...]
    unnamed x2 -> x0, local copies, waits for them, and re-layouts: 2.65 us -> none
    pallas_call x0 -> x1, Pallas kernels: none -> 1.48 us  [local(): pl.pallas_call(close, out_shape=(jax.ShapeDtypeStruct((qr, width), BF16),...]
where the time goes in v2:
time: 60.4 us; the launch traced here: 60.2 us
  Pallas kernels  59.5 us (99%)
  between operations  0.64 us (1%)
    pallas_call x1, Pallas kernels, local(): pl.pallas_call(kernel, out_shape=(jax.ShapeDtypeStruct((qr, width), BF16)...  58 us
    pallas_call x1, Pallas kernels, local(): pl.pallas_call(close, out_shape=(jax.ShapeDtypeStruct((qr, width), BF16),...  1.48 us

profile of v2, /device:TPU:1, one launch (start us, length us, event | category | flops | bytes accessed | tf_op | source)
XLA Modules:
  0.0 60.2 jit_solution(10944900630135927872)
XLA Ops:
  0.6 58.0 %sparse_attention.1 = (bf16[64,128]{1,0:T(8,128)(2,1)}, bf16[4,64,128]{2,1,0:T(8,128)(2,1)}) custom-call(bf16[64,128]{1,0:T(8,128)(2,1)} %bitcast.8, bf16[8,128]{1,0:T(8,128)(2,1)} %bitcast.9, bf16[8,128]{1,0:T(8,128)(2,1)} %bitcast.10, s32[16,12]{1,0:T(8,128)} %gat_ref.1, bf16[16384,128]{1,0:T(8,128)(2,1)} %bitcast.6, bf16[16384,128]{1,0:T(8,128)(2,1)} %bitcast.7, ...), custom_call_target="tpu_custom_call" | custom-call | tf_op jit(solution)/shard_map/sparse_attention/pallas_call | solution.py:523
  58.7 1.5 %close.1 = (bf16[64,128]{1,0:T(8,128)(2,1)}, bf16[64,128]{1,0:T(8,128)(2,1)}) custom-call(bf16[64,128]{1,0:T(8,128)(2,1)} %get-tuple-element.6.att_ref, bf16[4,64,128]{2,1,0:T(8,128)(2,1)} %get-tuple-element.7.part_ref), custom_call_target="tpu_custom_call" | custom-call | tf_op jit(solution)/shard_map/close/pallas_call | solution.py:535

commit v3 on v2

--- a/solution.py
+++ b/solution.py
@@ -39,16 +39,12 @@
         self.c = lax.rem(self.me, 2)
         self.z = lax.rem(lax.div(self.me, 2), Z)
         self.y = lax.div(self.me, 2 * Z)
-        self.zc = 2 * self.z + self.c
 
     def rank(self, dy, dz, dc):
         return (lax.rem(self.y + dy, Y) * Z + lax.rem(self.z + dz, Z)) * 2 + lax.rem(self.c + dc, 2)
 
     def y_of(self, dy):
         return lax.rem(self.y + dy, Y)
-
-    def zc_of(self, dz):
-        return 2 * lax.rem(self.z + dz, Z) + self.c
 
     def copy(self, ref, send, recv, dy, dz, dc):
         return pltpu.make_async_remote_copy(src_ref=ref, dst_ref=ref, send_sem=send, recv_sem=recv,
@@ -56,117 +52,90 @@
 
 
 class GatherZ:
-    def __init__(self, m, buf, at, zs, ys, cs, sends):
-        self.m, self.buf, self.at = m, buf, at
-        self.zs, self.ys, self.cs, self.sends = zs, ys, cs, sends
+    def __init__(self, m, buf, at, slot, zs, ys, sends, ahead=()):
+        self.m, self.buf, self.at, self.slot = m, buf, at, slot
+        self.zs, self.ys, self.sends = zs, ys, sends
+        self.ahead = ahead or far_first(Y)[:-1]
+
+    def ref(self, dy, dz):
+        return self.buf.at[self.m.y_of(dy), self.slot(dz), self.at]
 
     def spread(self, dz):
         m = self.m
-        ref = self.buf.at[m.y, m.zc_of(Z - dz), self.at]
-        for dy in far_first(Y)[:-1]:
-            m.copy(ref, self.sends.at[1], self.ys.at[dz, dy - 1], dy, 0, 0).start()
+        for dy in self.ahead:
+            m.copy(self.ref(0, Z - dz), self.sends.at[1], self.ys.at[dz, dy - 1], dy, 0, 0).start()
 
     def start(self):
         m = self.m
-        ref = self.buf.at[m.y, m.zc, self.at]
-        for dz in far_first(Z)[:-1]:
-            m.copy(ref, self.sends.at[0], self.zs.at[dz - 1], 0, dz, 0).start()
+        for dz in near_first(Z):
+            m.copy(self.ref(0, 0), self.sends.at[0], self.zs.at[dz - 1], 0, dz, 0).start()
         self.spread(0)
 
     def along_z(self, dz):
+        self.m.copy(self.ref(0, Z - dz), self.sends.at[0], self.zs.at[dz - 1], 0, dz, 0).wait_recv()
+        self.spread(dz)
+
+    def along_y(self, dy, dz):
+        self.m.copy(self.ref(dy, Z - dz), self.sends.at[1], self.ys.at[dz, Y - dy - 1], Y - dy, 0, 0).wait_recv()
+
+    def core(self, dy, dz, sem):
+        self.m.copy(self.ref(dy, Z - dz), self.sends.at[2], sem, 0, 0, 1).start()
+
+    def core_wait(self, number, sem):
+        shards = self.buf.at[pl.ds(0, number // Z), pl.ds(0, Z), self.at]
+        self.m.copy(shards, self.sends.at[2], sem, 0, 0, 1).wait_recv()
+
+    def drain(self, core):
         m = self.m
-        m.copy(self.buf.at[m.y, m.zc_of(Z - dz), self.at], self.sends.at[0], self.zs.at[dz - 1], 0, dz, 0).wait_recv()
-        self.spread(dz)
-
-    def along_y(self, dz):
-        m = self.m
-        zc = m.zc_of(Z - dz)
-        for dy in near_first(Y):
-            m.copy(self.buf.at[m.y_of(Y - dy), zc, self.at], self.sends.at[1], self.ys.at[dz, dy - 1], dy, 0, 0).wait_recv()
-        m.copy(self.buf.at[:, zc, self.at], self.sends.at[2], self.cs, 0, 0, 1).start()
-
-    def finish(self):
-        self.m.copy(self.buf.at[:, pl.ds(0, Z), self.at], self.sends.at[2], self.cs, 0, 0, 1).wait_recv()
-
-    def drain(self):
-        m = self.m
-        m.copy(self.buf.at[0, pl.ds(0, Z - 1), self.at], self.sends.at[0], self.cs, 0, 0, 1).wait_send()
-        m.copy(self.buf.at[pl.ds(0, Y - 1), pl.ds(0, Z), self.at], self.sends.at[1], self.cs, 0, 0, 1).wait_send()
-        m.copy(self.buf.at[:, pl.ds(0, Z), self.at], self.sends.at[2], self.cs, 0, 0, 1).wait_send()
+        parts = [self.buf.at[0, pl.ds(0, Z - 1), self.at], self.buf.at[pl.ds(0, Y - 1), pl.ds(0, Z), self.at]]
+        if core:
+            parts.append(self.buf.at[:, pl.ds(0, Z), self.at])
+        for i, part in enumerate(parts):
+            m.copy(part, self.sends.at[i], self.zs.at[0], 0, 0, 1).wait_send()
 
 
 class GatherY:
-    def __init__(self, m, buf, at, ys, zs, cs, sends):
-        self.m, self.buf, self.at = m, buf, at
-        self.ys, self.zs, self.cs, self.sends = ys, zs, cs, sends
+    def __init__(self, m, buf, at, slot, ys, zs, sends):
+        self.m, self.buf, self.at, self.slot = m, buf, at, slot
+        self.ys, self.zs, self.sends = ys, zs, sends
 
     def start(self):
         m = self.m
-        ref = self.buf.at[m.y, m.zc, self.at]
+        ref = self.buf.at[m.y, self.slot(0), self.at]
         for dy in far_first(Y)[:-1]:
             m.copy(ref, self.sends.at[0], self.ys.at[dy - 1], dy, 0, 0).start()
 
     def forward(self):
         m = self.m
         for dy in near_first(Y):
-            m.copy(self.buf.at[m.y_of(Y - dy), m.zc, self.at], self.sends.at[0], self.ys.at[dy - 1], dy, 0, 0).wait_recv()
-        ref = self.buf.at[:, m.zc, self.at]
+            ref = self.buf.at[m.y_of(Y - dy), self.slot(0), self.at]
+            m.copy(ref, self.sends.at[0], self.ys.at[dy - 1], dy, 0, 0).wait_recv()
         for dz in far_first(Z)[:-1]:
-            m.copy(ref, self.sends.at[1], self.zs.at[dz - 1], 0, dz, 0).start()
-        m.copy(ref, self.sends.at[2], self.cs, 0, 0, 1).start()
+            m.copy(self.buf.at[:, self.slot(0), self.at], self.sends.at[1], self.zs.at[dz - 1], 0, dz, 0).start()
 
     def across(self, dz):
-        m = self.m
-        ref = self.buf.at[:, m.zc_of(Z - dz), self.at]
-        m.copy(ref, self.sends.at[1], self.zs.at[dz - 1], 0, dz, 0).wait_recv()
-        m.copy(ref, self.sends.at[2], self.cs, 0, 0, 1).start()
-
-    def finish(self):
-        self.m.copy(self.buf.at[:, pl.ds(0, Z), self.at], self.sends.at[2], self.cs, 0, 0, 1).wait_recv()
+        ref = self.buf.at[:, self.slot(Z - dz), self.at]
+        self.m.copy(ref, self.sends.at[1], self.zs.at[dz - 1], 0, dz, 0).wait_recv()
 
     def drain(self):
         m = self.m
-        m.copy(self.buf.at[0, pl.ds(0, Y - 1), self.at], self.sends.at[0], self.cs, 0, 0, 1).wait_send()
-        m.copy(self.buf.at[:, pl.ds(0, Z - 1), self.at], self.sends.at[1], self.cs, 0, 0, 1).wait_send()
-        m.copy(self.buf.at[:, pl.ds(0, Z), self.at], self.sends.at[2], self.cs, 0, 0, 1).wait_send()
-
-
-class Gather:
-    def __init__(self, m, buf, sems):
-        rows = buf.shape[2]
-        cut = rows - rows // 4
-        self.a = GatherZ(m, buf, pl.ds(0, cut), *sems[:4])
-        self.b = GatherY(m, buf, pl.ds(cut, rows - cut), *sems[4:])
-
-    def run(self, beside):
-        a, b = self.a, self.b
-        b.start()
-        a.start()
-        near = near_first(Z)
-        for i, dz in enumerate(near):
-            beside()
-            a.along_z(dz)
-            if i == min(1, len(near) - 1):
-                b.forward()
-        beside()
-        a.along_y(0)
-        for dz in near:
-            beside()
-            a.along_y(dz)
-            b.across(dz)
-        a.finish()
-        b.finish()
-
-    def drain(self):
-        self.a.drain()
-        self.b.drain()
+        m.copy(self.buf.at[0, pl.ds(0, Y - 1), self.at], self.sends.at[0], self.zs.at[0], 0, 0, 1).wait_send()
+        m.copy(self.buf.at[:, pl.ds(0, Z - 1), self.at], self.sends.at[1], self.zs.at[0], 0, 0, 1).wait_send()
 
 
 def kernel(q_ref, sk_ref, sv_ref, gat_ref, kc_ref, vc_ref, w_ref, att_ref, part_ref,
            kraw, vraw, k0, k1, v0, v1, wv, buf, buf2, bufkv, f32s, kv32, d32, qaug,
            sb, cm, pb, alb, acc, mm, ll, ob, pf, pay, recv, own_o, own_l, xp,
-           loc, ar, asend, xs, xrs, *sems):
+           loc, ar, asend, xs, xrs, ws, wrs, c1, c3, *sems):
     m = Comm()
+    zc = 2 * m.z + m.c
+
+    def both_cores(dz):
+        return 2 * lax.rem(m.z + dz, Z) + m.c
+
+    def one_core(dz):
+        return lax.rem(m.z + dz, Z)
+
     n = Y * Z * 2
     me, kv = m.me, m.kv
     heads, topk = gat_ref.shape
@@ -183,20 +152,23 @@
 
     kcopy = pltpu.make_async_copy(kc_ref, kraw, loc.at[0])
     vcopy = pltpu.make_async_copy(vc_ref, vraw, loc.at[1])
-    wcopy = pltpu.make_async_copy(w_ref, wv, loc.at[2])
+    wcopy = pltpu.make_async_copy(w_ref, wv.at[m.c], loc.at[2])
+    wgive = pltpu.make_async_remote_copy(src_ref=w_ref, dst_ref=wv.at[m.c], send_sem=ws, recv_sem=wrs,
+                                         device_id=(m.rank(0, 0, 1), kv), device_id_type=MESH)
     bar = pltpu.get_barrier_semaphore()
     for dz in far_first(Z)[:-1]:
         pl.semaphore_signal(bar, inc=1, device_id=(m.rank(0, dz, 0), kv), device_id_type=MESH)
     for dy in far_first(Y)[:-1]:
         pl.semaphore_signal(bar, inc=1, device_id=(m.rank(dy, 0, 0), kv), device_id_type=MESH)
-    pl.semaphore_signal(bar, inc=1, device_id=(m.rank(0, 0, 1), kv), device_id_type=MESH)
-    for dx in range(1, X):
-        pl.semaphore_signal(bar, inc=1, device_id=(me, lax.rem(kv + dx, X)), device_id_type=MESH)
+    for dx in range(X):
+        for dc in range(2):
+            if (dx, dc) != (0, 0):
+                pl.semaphore_signal(bar, inc=1, device_id=(m.rank(0, 0, dc), lax.rem(kv + dx, X)), device_id_type=MESH)
     kcopy.start()
     vcopy.start()
     wcopy.start()
-    buf[m.y, m.zc] = q_ref[...]
-    bufkv[m.y, m.zc] = jnp.concatenate([sk_ref[...], sv_ref[...]], axis=0)
+    buf[m.y, zc] = q_ref[...]
+    bufkv[m.y, zc] = jnp.concatenate([sk_ref[...], sv_ref[...]], axis=0)
 
     lane = lax.broadcasted_iota(jnp.int32, (heads, 2 * n), 1)
     block_of = lax.rem(lane, n) * 2 + lax.div(lane, n)
@@ -237,32 +209,50 @@
 
     work = pieces()
     todo = 2 * parts
-    each = -(-todo // (2 * Z + 1))
+    each = -(-todo // (2 * Z))
 
     def beside():
         for _ in range(each):
             next(work, None)
 
     beside()
-    pl.semaphore_wait(bar, Z - 1 + Y - 1 + 1 + X - 1)
-    g1 = Gather(m, buf, sems[0:8])
-    g1.run(beside)
+    pl.semaphore_wait(bar, Z - 1 + Y - 1 + 2 * X - 1)
+
+    near = near_first(Z)
+    g1 = GatherZ(m, buf, pl.ds(0, qr), both_cores, sems[0], sems[1], sems[2], ahead=range(Y - 1, 0, -1))
+    g1.start()
+    g1.core(0, 0, c1.at[0])
+    for dz in near:
+        beside()
+        g1.along_z(dz)
+        g1.core(0, dz, c1.at[0])
+    first_half = list(range(1, Y // 2))
+    second_half = list(range(Y // 2, Y))
+    for dz in [0] + near:
+        beside()
+        for dy in first_half:
+            g1.along_y(dy, dz)
+            g1.core(dy, dz, c1.at[0])
     for _ in work:
         pass
-    g3 = GatherZ(m, bufkv, pl.ds(0, 2 * kvr), *sems[16:20])
+    g1.core_wait(Y * Z // 2, c1.at[0])
+    wgive.start()
+    g3 = GatherZ(m, bufkv, pl.ds(0, 2 * kvr), both_cores, sems[3], sems[4], sems[5])
     g3.start()
 
-    def widen(i, _):
-        zc = lax.rem(i, 2 * Z)
-        f32s[pl.ds(pl.multiple_of(i * qr, qr), qr), :] = buf[lax.div(i, 2 * Z), zc].astype(F32)
-        return 0
-
-    lax.fori_loop(0, n, widen, 0)
-
     nb = bp // CHUNK
-    far = far_first(Y)
     for half in range(2):
-        dys = far[half * (Y // 2):(half + 1) * (Y // 2)]
+        dys = list(range(half * (Y // 2), (half + 1) * (Y // 2)))
+        if half == 1:
+            g1.core_wait(Y * Z // 2, c1.at[1])
+        for dy in dys:
+            yy = m.y_of(dy)
+
+            def widen(i, _):
+                f32s[pl.ds(pl.multiple_of((yy * (2 * Z) + i) * qr, qr), qr), :] = buf[yy, i].astype(F32)
+                return 0
+
+            lax.fori_loop(0, 2 * Z, widen, 0)
         for b in range(2):
             for s in range(MOST):
                 h = own_heads[b][s]
@@ -332,18 +322,14 @@
                 stat = jnp.where((lax.rem(ln, 16) == s * rows + rw) & (ln < 48), val, stat)
             ob[MOST] = stat
             for t, dy in enumerate(dys):
-                to_y = m.y_of(dy) * (2 * Z)
-
-                def pack(j, _):
+                for j in range(Z):
+                    d = t * 2 * Z + 2 * j
                     for s in range(MOST + 1):
-                        x = ob[s, pl.ds(pl.multiple_of(t * row + j * 8, 8), 8), :]
-                        pf[s * rows:(s + 1) * rows, :] = x[0:rows]
-                        pf[16 + s * rows:16 + (s + 1) * rows, :] = x[rows:2 * rows]
-                    pay[b, to_y + 2 * j] = pf[0:16, :].astype(BF16)
-                    pay[b, to_y + 2 * j + 1] = pf[16:32, :].astype(BF16)
-                    return 0
-
-                lax.fori_loop(0, Z, pack, 0)
+                        x = ob[s, d * rows:(d + 2) * rows, :]
+                        pf[d * 16 + s * rows:d * 16 + (s + 1) * rows, :] = x[0:rows]
+                        pf[(d + 1) * 16 + s * rows:(d + 1) * 16 + (s + 1) * rows, :] = x[rows:2 * rows]
+                of_y = pf[t * 2 * Z * 16:(t + 1) * 2 * Z * 16, :].astype(BF16).reshape(2 * Z, 16, 128)
+                pay[b, pl.ds(m.y_of(dy) * (2 * Z), 2 * Z)] = of_y
             if 0 in dys:
                 recv[b, me] = pay[b, me]
 
@@ -365,19 +351,30 @@
                 for dc in range(2):
                     if (dy, dc) != (0, 0):
                         send(dy, 0, dc)
+            if half == 0:
+                @pl.when(b == 0)
+                def _():
+                    for dz in [0] + near:
+                        for dy in second_half:
+                            g1.along_y(dy, dz)
+                            g1.core(dy, dz, c1.at[1])
             return 0
 
         lax.fori_loop(0, 2, unit, 0)
         if half == 0:
-            for dz in near_first(Z):
+            g3.core(0, 0, c3)
+            for dz in near:
                 g3.along_z(dz)
-    for dz in range(Z):
-        g3.along_y(dz)
-    g3.finish()
+                g3.core(0, dz, c3)
+    for dz in [0] + near:
+        for dy in range(1, Y):
+            g3.along_y(dy, dz)
+            g3.core(dy, dz, c3)
+    g3.core_wait(Y * Z, c3)
 
     def widenkv(i, _):
-        zc = lax.rem(i, 2 * Z)
-        kv32[pl.ds(pl.multiple_of(i * 2 * kvr, 2 * kvr), 2 * kvr), :] = bufkv[lax.div(i, 2 * Z), zc].astype(F32)
+        kv32[pl.ds(pl.multiple_of(i * 2 * kvr, 2 * kvr), 2 * kvr), :] = (
+            bufkv[lax.div(i, 2 * Z), lax.rem(i, 2 * Z)].astype(F32))
         return 0
 
     lax.fori_loop(0, n, widenkv, 0)
@@ -435,56 +432,80 @@
             num = num + (two[0:heads] + two[heads:2 * heads])
         a = (num / den).astype(BF16)
         att_ref[at, :] = a
-        buf2[m.y, m.zc, at, :] = a
-
-    g2 = Gather(m, buf2, sems[8:16])
-    g2.run(lambda: None)
+        buf2[m.y, m.z, at, :] = a
+
+    cut = qr - qr // 4
+    g2 = GatherZ(m, buf2, pl.ds(0, cut), one_core, *sems[6:9])
+    g4 = GatherY(m, buf2, pl.ds(cut, qr - cut), one_core, *sems[9:12])
+    g4.start()
+    g2.start()
+    for i, dz in enumerate(near):
+        g2.along_z(dz)
+        if i == min(1, len(near) - 1):
+            g4.forward()
+    for dz in [0] + near:
+        for dy in range(1, Y):
+            g2.along_y(dy, dz)
+    for dz in near:
+        g4.across(dz)
     wcopy.wait()
-    share = np_ // X
-    per_x = n // X
+    wgive.wait()
+    share = Z * rows
     for dxs in (far_first(X)[:X // 2], far_first(X)[X // 2:]):
         for t, dx in enumerate(dxs):
             x = lax.rem(kv + dx, X)
-
-            def widen2(i, _):
-                j = x * per_x + i
-                to = pl.ds(pl.multiple_of((t * per_x + i) * qr, qr), qr)
-                f32s[to, :] = buf2[lax.div(j, 2 * Z), lax.rem(j, 2 * Z)].astype(F32)
-                return 0
-
-            lax.fori_loop(0, per_x, widen2, 0)
-        out = jnp.zeros((len(dxs) * share, 128), F32)
+            for j in range(Z):
+                f32s[(t * Z + j) * qr:(t * Z + j + 1) * qr, :] = buf2[x, j].astype(F32)
+        out = jnp.zeros((len(dxs) * share, 256), F32)
         for h in range(0, heads, 2):
             a = jnp.concatenate([f32s[pl.ds(h + e, len(dxs) * share, stride=heads), :] for e in range(2)], axis=1)
-            out = out + dot(a.astype(BF16), wv[h * width:(h + 2) * width, :])
+            at = slice(h * width, (h + 2) * width)
+            out = out + dot(a.astype(BF16), jnp.concatenate([wv[0, at, :], wv[1, at, :]], axis=1))
         for t, dx in enumerate(dxs):
             x = lax.rem(kv + dx, X)
-            piece = out[t * share:(t + 1) * share].astype(BF16)
-            if dx == 0:
-                part_ref[kv] = piece
-            else:
-                xp[dx - 1] = piece
-                pltpu.make_async_remote_copy(src_ref=xp.at[dx - 1], dst_ref=part_ref.at[kv], send_sem=xs.at[dx - 1],
-                                             recv_sem=xrs.at[dx - 1], device_id=(me, x), device_id_type=MESH).start()
-    g1.drain()
-    g2.drain()
-    g3.drain()
+            mine = out[t * share:(t + 1) * share]
+            halves = [mine[:, 0:128], mine[:, 128:256]]
+            for dc in range(2):
+                piece = jnp.where(lax.rem(m.c + dc, 2) == 0, halves[0], halves[1]).astype(BF16)
+                if (dx, dc) == (0, 0):
+                    part_ref[kv, m.c] = piece
+                else:
+                    k = 2 * dx + dc - 1
+                    xp[k] = piece
+                    pltpu.make_async_remote_copy(
+                        src_ref=xp.at[k], dst_ref=part_ref.at[kv, m.c], send_sem=xs.at[k], recv_sem=xrs.at[k],
+                        device_id=(m.rank(0, 0, dc), x), device_id_type=MESH).start()
+    g1.drain(True)
+    g3.drain(True)
+    g2.drain(False)
+    g4.drain()
     for b in range(2):
         rest = pay.at[b, pl.ds(0, n - 1)]
         pltpu.make_async_remote_copy(src_ref=rest, dst_ref=rest, send_sem=asend, recv_sem=ar.at[b],
                                      device_id=(m.rank(0, 1, 0), kv), device_id_type=MESH).wait_send()
-    for dx in range(1, X):
-        pltpu.make_async_remote_copy(src_ref=xp.at[dx - 1], dst_ref=part_ref.at[lax.rem(kv + X - dx, X)],
-                                     send_sem=xs.at[dx - 1], recv_sem=xrs.at[dx - 1],
-                                     device_id=(me, lax.rem(kv + dx, X)), device_id_type=MESH).wait()
+    for dx in range(X):
+        for dc in range(2):
+            if (dx, dc) != (0, 0):
+                k = 2 * dx + dc - 1
+                pltpu.make_async_remote_copy(
+                    src_ref=xp.at[k], dst_ref=part_ref.at[lax.rem(kv + X - dx, X), lax.rem(m.c + dc, 2)],
+                    send_sem=xs.at[k], recv_sem=xrs.at[k],
+                    device_id=(m.rank(0, 0, dc), lax.rem(kv + dx, X)), device_id_type=MESH).wait()
 
 
 def close(att_ref, part_ref, a_ref, p_ref):
     a_ref[...] = att_ref[...]
-    total = part_ref[0].astype(F32)
-    for x in range(1, X):
-        total = total + part_ref[x].astype(F32)
-    p_ref[...] = total.astype(BF16)
+    rows = p_ref.shape[0]
+    sums = []
+    for c in range(2):
+        total = part_ref[0, c].astype(F32)
+        for x in range(1, X):
+            total = total + part_ref[x, c].astype(F32)
+        sums.append(total.reshape(rows // 16, 8, 128))
+    low = lax.broadcasted_iota(jnp.int32, sums[0].shape, 1) < 4
+    even = jnp.where(low, sums[0], pltpu.roll(sums[1], 4, 1))
+    odd = jnp.where(low, pltpu.roll(sums[0], 4, 1), sums[1])
+    p_ref[...] = jnp.stack([even, odd], axis=1).reshape(rows, 128).astype(BF16)
 
 
 def local(queries, span_keys, span_values, cache_keys, cache_values, gating, out_weight):
@@ -500,29 +521,29 @@
     unit = MOST * np_ // 2
     vm = pltpu.VMEM
     dma = pltpu.SemaphoreType.DMA
-    along = [dma((Z - 1,)), dma((Z, Y - 1)), dma, dma((3,))]
-    both = along + [dma((Y - 1,)), dma((Z - 1,)), dma, dma((3,))]
+    along_z = [dma((Z - 1,)), dma((Z, Y - 1)), dma((3,))]
+    along_y = [dma((Y - 1,)), dma((Z - 1,)), dma((3,))]
     scratch = [
         vm((raw, width), BF16), vm((raw, width), BF16),
         vm((2 * bp, width), BF16), vm((2 * bp, width), BF16), vm((2 * bp, width), BF16), vm((2 * bp, width), BF16),
-        vm(out_weight.shape, BF16),
-        vm((Y, 2 * Z, qr, width), BF16), vm((Y, 2 * Z, qr, width), BF16), vm((Y, 2 * Z, 2 * kvr, width), BF16),
+        vm((2, *out_weight.shape), BF16),
+        vm((Y, 2 * Z, qr, width), BF16), vm((Y, Z, qr, width), BF16), vm((Y, 2 * Z, 2 * kvr, width), BF16),
         vm((n * qr, width), F32), vm((n * 2 * kvr, width), F32), vm((part, width), F32),
         vm((2, unit, 2 * width), BF16),
         vm((2, unit, CHUNK), F32), vm((2, unit, width), F32), vm((2, unit, CHUNK), BF16), vm((2, unit, width), F32),
         vm((unit, 2 * width), F32), vm((unit, width), F32), vm((unit, width), F32),
-        vm((MOST + 1, np_ // 2, width), F32), vm((32, width), F32),
+        vm((MOST + 1, np_ // 2, width), F32), vm((n // 2 * 16, width), F32),
         vm((2, n, 16, width), BF16), vm((2, n, 16, width), BF16),
         vm((qr, width), F32), vm((qr, width), F32),
-        vm((X - 1, np_ // X, width), BF16),
-        dma((3,)), dma((2,)), dma, dma((X - 1,)), dma((X - 1,)),
-        *both, *both, *along,
+        vm((2 * X - 1, Z * rows, width), BF16),
+        dma((3,)), dma((2,)), dma, dma((2 * X - 1,)), dma((2 * X - 1,)), dma, dma, dma((2,)), dma,
+        *along_z, *along_z, *along_z, *along_y,
     ]
     inv = pl.BlockSpec(memory_space=pltpu.VMEM)
     anyw = pl.BlockSpec(memory_space=pl.ANY)
     att, parts = pl.pallas_call(
         kernel,
-        out_shape=(jax.ShapeDtypeStruct((qr, width), BF16), jax.ShapeDtypeStruct((X, np_ // X, width), BF16)),
+        out_shape=(jax.ShapeDtypeStruct((qr, width), BF16), jax.ShapeDtypeStruct((X, 2, Z * rows, width), BF16)),
         in_specs=[inv, inv, inv, inv, anyw, anyw, anyw],
         out_specs=(inv, inv),
         scratch_shapes=scratch,

time: 60.4 us -> 59.2 us (0.980)
  Pallas kernels: 59.5 us -> 58.3 us
    pallas_call x1, Pallas kernels: 58 us -> 56.9 us  [local(): pl.pallas_call(kernel, out_shape=(jax.ShapeDtypeStruct((qr, width), BF16)...]
where the time goes in v3:
time: 59.2 us; the launch traced here: 59 us
  Pallas kernels  58.3 us (98%)
  between operations  0.64 us (1%)
    pallas_call x1, Pallas kernels, local(): pl.pallas_call(kernel, out_shape=(jax.ShapeDtypeStruct((qr, width), BF16)...  56.9 us
    pallas_call x1, Pallas kernels, local(): pl.pallas_call(close, out_shape=(jax.ShapeDtypeStruct((qr, width), BF16),...  1.48 us

profile of v3, /device:TPU:1, one launch (start us, length us, event | category | flops | bytes accessed | tf_op | source)
XLA Modules:
  0.0 59.0 jit_solution(9260875695664829025)
XLA Ops:
  0.6 56.9 %sparse_attention.1 = (bf16[64,128]{1,0:T(8,128)(2,1)}, bf16[4,2,32,128]{3,2,1,0:T(8,128)(2,1)}) custom-call(bf16[64,128]{1,0:T(8,128)(2,1)} %bitcast.8, bf16[8,128]{1,0:T(8,128)(2,1)} %bitcast.9, bf16[8,128]{1,0:T(8,128)(2,1)} %bitcast.10, s32[16,12]{1,0:T(8,128)} %gat_ref.1, bf16[16384,128]{1,0:T(8,128)(2,1)} %bitcast.6, bf16[16384,128]{1,0:T(8,128)(2,1)} %bitcast.7, ...), custom_call_target="tpu_custom_call" | custom-call | tf_op jit(solution)/shard_map/sparse_attention/pallas_call | solution.py:544
  57.5 1.5 %close.1 = (bf16[64,128]{1,0:T(8,128)(2,1)}, bf16[64,128]{1,0:T(8,128)(2,1)}) custom-call(bf16[64,128]{1,0:T(8,128)(2,1)} %get-tuple-element.6.att_ref, bf16[4,2,32,128]{3,2,1,0:T(8,128)(2,1)} %get-tuple-element.7.part_ref), custom_call_target="tpu_custom_call" | custom-call | tf_op jit(solution)/shard_map/close/pallas_call | solution.py:556

commit v4 on v3

--- a/solution.py
+++ b/solution.py
@@ -10,7 +10,7 @@
 Y, Z, X = 4, 8, 4
 BLOCK_POSITIONS = 4096
 MOST = 3
-CHUNK = 1024
+CHUNK = 2048
 NEG = -1e30
 MESH = pl.DeviceIdType.MESH
 F32, BF16 = jnp.float32, jnp.bfloat16
@@ -126,7 +126,7 @@
 def kernel(q_ref, sk_ref, sv_ref, gat_ref, kc_ref, vc_ref, w_ref, att_ref, part_ref,
            kraw, vraw, k0, k1, v0, v1, wv, buf, buf2, bufkv, f32s, kv32, d32, qaug,
            sb, cm, pb, alb, acc, mm, ll, ob, pf, pay, recv, own_o, own_l, xp,
-           loc, ar, asend, xs, xrs, ws, wrs, c1, c3, *sems):
+           loc, wl, ar, asend, xs, xrs, ws, wrs, c1, c3, *sems):
     m = Comm()
     zc = 2 * m.z + m.c
 
@@ -150,9 +150,7 @@
     hp = Y // 2 * row
     c2s = width ** -0.5 * 1.4426950408889634
 
-    kcopy = pltpu.make_async_copy(kc_ref, kraw, loc.at[0])
-    vcopy = pltpu.make_async_copy(vc_ref, vraw, loc.at[1])
-    wcopy = pltpu.make_async_copy(w_ref, wv.at[m.c], loc.at[2])
+    wcopy = pltpu.make_async_copy(w_ref, wv.at[m.c], wl)
     wgive = pltpu.make_async_remote_copy(src_ref=w_ref, dst_ref=wv.at[m.c], send_sem=ws, recv_sem=wrs,
                                          device_id=(m.rank(0, 0, 1), kv), device_id_type=MESH)
     bar = pltpu.get_barrier_semaphore()
@@ -164,9 +162,6 @@
         for dc in range(2):
             if (dx, dc) != (0, 0):
                 pl.semaphore_signal(bar, inc=1, device_id=(m.rank(0, 0, dc), lax.rem(kv + dx, X)), device_id_type=MESH)
-    kcopy.start()
-    vcopy.start()
-    wcopy.start()
     buf[m.y, zc] = q_ref[...]
     bufkv[m.y, zc] = jnp.concatenate([sk_ref[...], sv_ref[...]], axis=0)
 
@@ -189,63 +184,64 @@
 
     part = d32.shape[0]
     parts = kraw.shape[0] // part
-
-    def split(raw, even, odd, i):
+    order = [(a, blk * (parts // 2) + i) for blk in range(2) for a in range(2) for i in range(parts // 2)]
+    arrays = ((kc_ref, kraw, k0, k1), (vc_ref, vraw, v0, v1))
+
+    def load(j):
+        a, i = order[j]
         at = pl.ds(i * part, part)
-        to = pl.ds(i * (part // 2), part // 2)
-        d32[...] = raw[at, :].astype(F32)
-        even[to, :] = d32[pl.ds(0, part // 2, stride=2), :].astype(BF16)
-        odd[to, :] = d32[pl.ds(1, part // 2, stride=2), :].astype(BF16)
+        return pltpu.make_async_copy(arrays[a][0].at[at], arrays[a][1].at[at], loc.at[j])
 
     def pieces():
-        kcopy.wait()
-        for i in range(parts):
-            split(kraw, k0, k1, i)
+        for j, (a, i) in enumerate(order):
+            load(j).wait()
+            _, raw, even, odd = arrays[a]
+            to = pl.ds(i * (part // 2), part // 2)
+            d32[...] = raw[pl.ds(i * part, part), :].astype(F32)
+            even[to, :] = d32[pl.ds(0, part // 2, stride=2), :].astype(BF16)
+            odd[to, :] = d32[pl.ds(1, part // 2, stride=2), :].astype(BF16)
             yield
-        vcopy.wait()
-        for i in range(parts):
-            split(vraw, v0, v1, i)
-            yield
 
     work = pieces()
-    todo = 2 * parts
-    each = -(-todo // (2 * Z))
-
-    def beside():
-        for _ in range(each):
+
+    def beside(number):
+        for _ in range(number):
             next(work, None)
 
-    beside()
+    for j in range(len(order)):
+        load(j).start()
+    beside(2)
     pl.semaphore_wait(bar, Z - 1 + Y - 1 + 2 * X - 1)
 
     near = near_first(Z)
     g1 = GatherZ(m, buf, pl.ds(0, qr), both_cores, sems[0], sems[1], sems[2], ahead=range(Y - 1, 0, -1))
     g1.start()
     g1.core(0, 0, c1.at[0])
+    beside(len(order) * 3 // 8)
     for dz in near:
-        beside()
         g1.along_z(dz)
         g1.core(0, dz, c1.at[0])
     first_half = list(range(1, Y // 2))
     second_half = list(range(Y // 2, Y))
+    beside(len(order) * 3 // 8)
     for dz in [0] + near:
-        beside()
         for dy in first_half:
             g1.along_y(dy, dz)
             g1.core(dy, dz, c1.at[0])
-    for _ in work:
-        pass
+    beside(len(order))
+    wcopy.start()
     g1.core_wait(Y * Z // 2, c1.at[0])
     wgive.start()
     g3 = GatherZ(m, bufkv, pl.ds(0, 2 * kvr), both_cores, sems[3], sems[4], sems[5])
     g3.start()
 
     nb = bp // CHUNK
-    for half in range(2):
-        dys = list(range(half * (Y // 2), (half + 1) * (Y // 2)))
-        if half == 1:
-            g1.core_wait(Y * Z // 2, c1.at[1])
-        for dy in dys:
+
+    def rows_of(half):
+        return list(range(half * (Y // 2), (half + 1) * (Y // 2)))
+
+    def prepare(half):
+        for dy in rows_of(half):
             yy = m.y_of(dy)
 
             def widen(i, _):
@@ -257,111 +253,123 @@
             for s in range(MOST):
                 h = own_heads[b][s]
                 first = (h < per).astype(F32)
-                for t, dy in enumerate(dys):
+                for t, dy in enumerate(rows_of(half)):
                     qh = f32s[pl.ds(m.y_of(dy) * (row * heads) + h, row, stride=heads), :]
-                    qaug[b, s * hp + t * row:s * hp + (t + 1) * row, :] = jnp.concatenate(
+                    qaug[2 * half + b, s * hp + t * row:s * hp + (t + 1) * row, :] = jnp.concatenate(
                         [qh * first, qh * (1.0 - first)], axis=1).astype(BF16)
 
-        def unit(b, _):
-            def both(even, odd, i):
-                at = pl.ds(pl.multiple_of(b * bp + i * CHUNK, CHUNK), CHUNK)
-                return jnp.concatenate([even[at, :], odd[at, :]], axis=1)
-
-            def score(slot, i):
-                s = dot_t(qaug[b], both(k0, k1, i))
-                sb[slot] = s
-                top = s[:, :128]
-                for j in range(1, CHUNK // 128):
-                    top = jnp.maximum(top, s[:, j * 128:(j + 1) * 128])
-                cm[slot] = top
-
-            def soften(slot):
-                m0 = mm[...]
-                m1 = jnp.maximum(m0, jnp.max(cm[slot], axis=1, keepdims=True) * c2s)
-                p = jnp.exp2(sb[slot] * c2s - m1[:, :1])
-                al = jnp.exp2(m0 - m1)
-                ps = p[:, :128]
-                for j in range(1, CHUNK // 128):
-                    ps = ps + p[:, j * 128:(j + 1) * 128]
-                ll[...] = ll[...] * al + ps
-                mm[...] = m1
-                alb[slot] = al
-                pb[slot] = p.astype(BF16)
-
-            def gain(slot, i):
-                al = alb[slot]
-                acc[...] = acc[...] * jnp.concatenate([al, al], axis=1) + dot(pb[slot], both(v0, v1, i))
-
-            acc[...] = jnp.zeros_like(acc)
-            ll[...] = jnp.zeros_like(ll)
-            mm[...] = jnp.full_like(mm, NEG)
-            score(0, 0)
-            score(1, 1)
-            soften(0)
-            for i in range(1, nb - 1):
-                score((i + 1) % 2, i + 1)
-                gain((i - 1) % 2, i - 1)
-                soften(i % 2)
-            gain(nb % 2, nb - 2)
-            soften((nb - 1) % 2)
-            gain((nb - 1) % 2, nb - 1)
-
-            ln = lax.broadcasted_iota(jnp.int32, (hp, 128), 1)
-            rw = lax.rem(lax.broadcasted_iota(jnp.int32, (hp, 128), 0), rows)
-            stat = jnp.zeros((hp, 128), F32)
-            for s in range(MOST):
-                sl = pl.ds(s * hp, hp)
-                tot = jnp.sum(ll[sl, :], axis=1, keepdims=True)
-                lse = mm[sl, :] + jnp.log2(tot)
-                first = jnp.where(b == 0, own_heads[0][s], own_heads[1][s]) < per
-                ob[s] = jnp.where(first, acc[sl, 0:128], acc[sl, 128:256]) * (1.0 / tot)
-                hi = lse.astype(BF16).astype(F32)
-                mid = (lse - hi).astype(BF16).astype(F32)
-                lo = (lse - hi) - mid
-                val = jnp.where(ln < 16, hi, jnp.where(ln < 32, mid, lo))
-                stat = jnp.where((lax.rem(ln, 16) == s * rows + rw) & (ln < 48), val, stat)
-            ob[MOST] = stat
-            for t, dy in enumerate(dys):
-                for j in range(Z):
-                    d = t * 2 * Z + 2 * j
-                    for s in range(MOST + 1):
-                        x = ob[s, d * rows:(d + 2) * rows, :]
-                        pf[d * 16 + s * rows:d * 16 + (s + 1) * rows, :] = x[0:rows]
-                        pf[(d + 1) * 16 + s * rows:(d + 1) * 16 + (s + 1) * rows, :] = x[rows:2 * rows]
-                of_y = pf[t * 2 * Z * 16:(t + 1) * 2 * Z * 16, :].astype(BF16).reshape(2 * Z, 16, 128)
-                pay[b, pl.ds(m.y_of(dy) * (2 * Z), 2 * Z)] = of_y
-            if 0 in dys:
-                recv[b, me] = pay[b, me]
-
-            def send(dy, dz, dc):
-                to = m.rank(dy, dz, dc)
-                pltpu.make_async_remote_copy(src_ref=pay.at[b, to], dst_ref=recv.at[b, me], send_sem=asend,
-                                             recv_sem=ar.at[b], device_id=(to, kv), device_id_type=MESH).start()
-
-            def sends(i, _):
-                k = lax.div(i + 1, 2)
-                dz = Z // 2 + jnp.where(lax.rem(i, 2) == 1, -k, k)
-                for dy in dys:
-                    for dc in range(2):
-                        send(dy, dz, dc)
-                return 0
-
-            lax.fori_loop(0, Z - 1, sends, 0)
+    def both(even, odd, g):
+        at = pl.ds((g // nb % 2) * bp + g % nb * CHUNK, CHUNK)
+        return jnp.concatenate([even[at, :], odd[at, :]], axis=1)
+
+    def score(g):
+        s = dot_t(qaug[g // nb], both(k0, k1, g))
+        sb[g % 2] = s
+        top = s[:, :128]
+        for j in range(1, CHUNK // 128):
+            top = jnp.maximum(top, s[:, j * 128:(j + 1) * 128])
+        cm[g % 2] = top
+
+    def soften(g):
+        u, slot = g // nb % 2, g % 2
+        m1 = jnp.max(cm[slot], axis=1, keepdims=True) * c2s
+        if g % nb:
+            m0 = mm[u]
+            m1 = jnp.maximum(m0, m1)
+            al = jnp.exp2(m0 - m1)
+            alb[slot] = al
+        else:
+            m1 = jnp.broadcast_to(m1, (MOST * hp, 128))
+        p = jnp.exp2(sb[slot] * c2s - m1[:, :1])
+        ps = p[:, :128]
+        for j in range(1, CHUNK // 128):
+            ps = ps + p[:, j * 128:(j + 1) * 128]
+        ll[u] = ll[u] * al + ps if g % nb else ps
+        mm[u] = m1
+        pb[slot] = p.astype(BF16)
+
+    def gain(g):
+        u, slot = g // nb % 2, g % 2
+        o = dot(pb[slot], both(v0, v1, g))
+        if g % nb:
+            al = alb[slot]
+            acc[u] = acc[u] * jnp.concatenate([al, al], axis=1) + o
+        else:
+            acc[u] = o
+
+    def pack(unit):
+        u, b = unit % 2, unit % 2
+        ln = lax.broadcasted_iota(jnp.int32, (hp, 128), 1)
+        rw = lax.rem(lax.broadcasted_iota(jnp.int32, (hp, 128), 0), rows)
+        stat = jnp.zeros((hp, 128), F32)
+        for s in range(MOST):
+            sl = pl.ds(s * hp, hp)
+            tot = jnp.sum(ll[u, sl, :], axis=1, keepdims=True)
+            lse = mm[u, sl, :] + jnp.log2(tot)
+            first = own_heads[b][s] < per
+            ob[s] = jnp.where(first, acc[u, sl, 0:128], acc[u, sl, 128:256]) * (1.0 / tot)
+            hi = lse.astype(BF16).astype(F32)
+            mid = (lse - hi).astype(BF16).astype(F32)
+            lo = (lse - hi) - mid
+            val = jnp.where(ln < 16, hi, jnp.where(ln < 32, mid, lo))
+            stat = jnp.where((lax.rem(ln, 16) == s * rows + rw) & (ln < 48), val, stat)
+        ob[MOST] = stat
+        for t, dy in enumerate(rows_of(unit // 2)):
+            for j in range(Z):
+                d = t * 2 * Z + 2 * j
+                for s in range(MOST + 1):
+                    x = ob[s, d * rows:(d + 2) * rows, :]
+                    pf[d * 16 + s * rows:d * 16 + (s + 1) * rows, :] = x[0:rows]
+                    pf[(d + 1) * 16 + s * rows:(d + 1) * 16 + (s + 1) * rows, :] = x[rows:2 * rows]
+            of_y = pf[t * 2 * Z * 16:(t + 1) * 2 * Z * 16, :].astype(BF16).reshape(2 * Z, 16, 128)
+            pay[b, pl.ds(m.y_of(dy) * (2 * Z), 2 * Z)] = of_y
+        if unit // 2 == 0:
+            recv[b, me] = pay[b, me]
+
+    def give(unit):
+        b = unit % 2
+        dys = rows_of(unit // 2)
+
+        def send(dy, dz, dc):
+            to = m.rank(dy, dz, dc)
+            pltpu.make_async_remote_copy(src_ref=pay.at[b, to], dst_ref=recv.at[b, me], send_sem=asend,
+                                         recv_sem=ar.at[b], device_id=(to, kv), device_id_type=MESH).start()
+
+        def sends(i, _):
+            k = lax.div(i + 1, 2)
+            dz = Z // 2 + jnp.where(lax.rem(i, 2) == 1, -k, k)
             for dy in dys:
                 for dc in range(2):
-                    if (dy, dc) != (0, 0):
-                        send(dy, 0, dc)
-            if half == 0:
-                @pl.when(b == 0)
-                def _():
-                    for dz in [0] + near:
-                        for dy in second_half:
-                            g1.along_y(dy, dz)
-                            g1.core(dy, dz, c1.at[1])
+                    send(dy, dz, dc)
             return 0
 
-        lax.fori_loop(0, 2, unit, 0)
-        if half == 0:
+        lax.fori_loop(0, Z - 1, sends, 0)
+        for dy in dys:
+            for dc in range(2):
+                if (dy, dc) != (0, 0):
+                    send(dy, 0, dc)
+
+    prepare(0)
+    score(0)
+    for g in range(4 * nb + 1):
+        if g + 1 == 2 * nb:
+            g1.core_wait(Y * Z // 2, c1.at[1])
+            prepare(1)
+        if g < 4 * nb:
+            soften(g)
+        if g >= 1:
+            gain(g - 1)
+        if g + 1 < 4 * nb:
+            score(g + 1)
+        if g >= 1 and g % nb == 0:
+            pack(g // nb - 1)
+            give(g // nb - 1)
+        if g == nb - 1:
+            for dz in [0] + near:
+                for dy in second_half:
+                    g1.along_y(dy, dz)
+                    g1.core(dy, dz, c1.at[1])
+        if g == 2 * nb:
             g3.core(0, 0, c3)
             for dz in near:
                 g3.along_z(dz)
@@ -517,7 +525,7 @@
     kvr = rows * groups
     bp = BLOCK_POSITIONS
     raw = 2 * bp * groups
-    part = min(1024, raw)
+    part = min(1024, raw // 2)
     unit = MOST * np_ // 2
     vm = pltpu.VMEM
     dma = pltpu.SemaphoreType.DMA
@@ -529,14 +537,14 @@
         vm((2, *out_weight.shape), BF16),
         vm((Y, 2 * Z, qr, width), BF16), vm((Y, Z, qr, width), BF16), vm((Y, 2 * Z, 2 * kvr, width), BF16),
         vm((n * qr, width), F32), vm((n * 2 * kvr, width), F32), vm((part, width), F32),
-        vm((2, unit, 2 * width), BF16),
+        vm((4, unit, 2 * width), BF16),
         vm((2, unit, CHUNK), F32), vm((2, unit, width), F32), vm((2, unit, CHUNK), BF16), vm((2, unit, width), F32),
-        vm((unit, 2 * width), F32), vm((unit, width), F32), vm((unit, width), F32),
+        vm((2, unit, 2 * width), F32), vm((2, unit, width), F32), vm((2, unit, width), F32),
         vm((MOST + 1, np_ // 2, width), F32), vm((n // 2 * 16, width), F32),
         vm((2, n, 16, width), BF16), vm((2, n, 16, width), BF16),
         vm((qr, width), F32), vm((qr, width), F32),
         vm((2 * X - 1, Z * rows, width), BF16),
-        dma((3,)), dma((2,)), dma, dma((2 * X - 1,)), dma((2 * X - 1,)), dma, dma, dma((2,)), dma,
+        dma((2 * (raw // part),)), dma, dma((2,)), dma, dma((2 * X - 1,)), dma((2 * X - 1,)), dma, dma, dma((2,)), dma,
         *along_z, *along_z, *along_z, *along_y,
     ]
     inv = pl.BlockSpec(memory_space=pltpu.VMEM)

time: 59.2 us -> 60.4 us (1.020)
  Pallas kernels: 58.3 us -> 59.5 us
    pallas_call x1, Pallas kernels: 56.9 us -> 58.1 us  [local(): pl.pallas_call(kernel, out_shape=(jax.ShapeDtypeStruct((qr, width), BF16)...]
where the time goes in v4:
time: 60.4 us; the launch traced here: 60.2 us
  Pallas kernels  59.5 us (99%)
  between operations  0.64 us (1%)
    pallas_call x1, Pallas kernels, local(): pl.pallas_call(kernel, out_shape=(jax.ShapeDtypeStruct((qr, width), BF16)...  58.1 us
    pallas_call x1, Pallas kernels, local(): pl.pallas_call(close, out_shape=(jax.ShapeDtypeStruct((qr, width), BF16),...  1.48 us

profile of v4, /device:TPU:1, one launch (start us, length us, event | category | flops | bytes accessed | tf_op | source)
XLA Modules:
  0.0 60.2 jit_solution(14656544131620251140)
XLA Ops:
  0.6 58.1 %sparse_attention.1 = (bf16[64,128]{1,0:T(8,128)(2,1)}, bf16[4,2,32,128]{3,2,1,0:T(8,128)(2,1)}) custom-call(bf16[64,128]{1,0:T(8,128)(2,1)} %bitcast.8, bf16[8,128]{1,0:T(8,128)(2,1)} %bitcast.9, bf16[8,128]{1,0:T(8,128)(2,1)} %bitcast.10, s32[16,12]{1,0:T(8,128)} %gat_ref.1, bf16[16384,128]{1,0:T(8,128)(2,1)} %bitcast.6, bf16[16384,128]{1,0:T(8,128)(2,1)} %bitcast.7, ...), custom_call_target="tpu_custom_call" | custom-call | tf_op jit(solution)/shard_map/sparse_attention/pallas_call | solution.py:552
  58.7 1.5 %close.1 = (bf16[64,128]{1,0:T(8,128)(2,1)}, bf16[64,128]{1,0:T(8,128)(2,1)}) custom-call(bf16[64,128]{1,0:T(8,128)(2,1)} %get-tuple-element.6.att_ref, bf16[4,2,32,128]{3,2,1,0:T(8,128)(2,1)} %get-tuple-element.7.part_ref), custom_call_target="tpu_custom_call" | custom-call | tf_op jit(solution)/shard_map/close/pallas_call | solution.py:564

commit v5 on v4

--- a/solution.py
+++ b/solution.py
@@ -10,7 +10,7 @@
 Y, Z, X = 4, 8, 4
 BLOCK_POSITIONS = 4096
 MOST = 3
-CHUNK = 2048
+CHUNK = 1024
 NEG = -1e30
 MESH = pl.DeviceIdType.MESH
 F32, BF16 = jnp.float32, jnp.bfloat16
@@ -124,9 +124,9 @@
 
 
 def kernel(q_ref, sk_ref, sv_ref, gat_ref, kc_ref, vc_ref, w_ref, att_ref, part_ref,
-           kraw, vraw, k0, k1, v0, v1, wv, buf, buf2, bufkv, f32s, kv32, d32, qaug,
+           kraw, vraw, k0, k1, v0, v1, wv, qpay, qrecv, buf2, bufkv, f32s, kv32, d32, qaug,
            sb, cm, pb, alb, acc, mm, ll, ob, pf, pay, recv, own_o, own_l, xp,
-           loc, wl, ar, asend, xs, xrs, ws, wrs, c1, c3, *sems):
+           loc, wl, ar, asend, xs, xrs, ws, wrs, qs, qrs, c3, *sems):
     m = Comm()
     zc = 2 * m.z + m.c
 
@@ -154,15 +154,15 @@
     wgive = pltpu.make_async_remote_copy(src_ref=w_ref, dst_ref=wv.at[m.c], send_sem=ws, recv_sem=wrs,
                                          device_id=(m.rank(0, 0, 1), kv), device_id_type=MESH)
     bar = pltpu.get_barrier_semaphore()
-    for dz in far_first(Z)[:-1]:
-        pl.semaphore_signal(bar, inc=1, device_id=(m.rank(0, dz, 0), kv), device_id_type=MESH)
-    for dy in far_first(Y)[:-1]:
-        pl.semaphore_signal(bar, inc=1, device_id=(m.rank(dy, 0, 0), kv), device_id_type=MESH)
-    for dx in range(X):
+
+    def greet(i, _):
+        pl.semaphore_signal(bar, inc=1, device_id=(lax.rem(me + i, n), kv), device_id_type=MESH)
+        return 0
+
+    lax.fori_loop(1, n, greet, 0)
+    for dx in range(1, X):
         for dc in range(2):
-            if (dx, dc) != (0, 0):
-                pl.semaphore_signal(bar, inc=1, device_id=(m.rank(0, 0, dc), lax.rem(kv + dx, X)), device_id_type=MESH)
-    buf[m.y, zc] = q_ref[...]
+            pl.semaphore_signal(bar, inc=1, device_id=(m.rank(0, 0, dc), lax.rem(kv + dx, X)), device_id_type=MESH)
     bufkv[m.y, zc] = jnp.concatenate([sk_ref[...], sv_ref[...]], axis=0)
 
     lane = lax.broadcasted_iota(jnp.int32, (heads, 2 * n), 1)
@@ -210,56 +210,72 @@
 
     for j in range(len(order)):
         load(j).start()
-    beside(2)
-    pl.semaphore_wait(bar, Z - 1 + Y - 1 + 2 * X - 1)
-
+    f32s[0:2 * n * 16, :] = jnp.zeros((2 * n * 16, 128), F32)
+    spot = lax.broadcasted_iota(jnp.int32, (128, 2 * n), 0)
+    q_all = jnp.concatenate([q_ref[...], jnp.zeros((128 - qr, width), BF16)], axis=0)
+    for s in range(MOST):
+        for i in range(rows):
+            pick = (spot == hm[s] + i * heads) & (hm[s] >= 0)
+            f32s[pl.ds(s * rows + i, 2 * n, stride=16), :] = dot(pick.astype(F32).T.astype(BF16), q_all)
+    for b in range(2):
+        qpay[b] = f32s[b * n * 16:(b + 1) * n * 16, :].astype(BF16).reshape(n, 16, 128)
+        qrecv[b, me] = qpay[b, me]
+    pl.semaphore_wait(bar, n - 1 + 2 * (X - 1))
     near = near_first(Z)
-    g1 = GatherZ(m, buf, pl.ds(0, qr), both_cores, sems[0], sems[1], sems[2], ahead=range(Y - 1, 0, -1))
-    g1.start()
-    g1.core(0, 0, c1.at[0])
-    beside(len(order) * 3 // 8)
-    for dz in near:
-        g1.along_z(dz)
-        g1.core(0, dz, c1.at[0])
-    first_half = list(range(1, Y // 2))
-    second_half = list(range(Y // 2, Y))
-    beside(len(order) * 3 // 8)
-    for dz in [0] + near:
-        for dy in first_half:
-            g1.along_y(dy, dz)
-            g1.core(dy, dz, c1.at[0])
+
+    def to_all(b, dys, source, target, send_sem, recv_sem):
+        def send(dy, dz, dc):
+            to = m.rank(dy, dz, dc)
+            pltpu.make_async_remote_copy(src_ref=source.at[b, to], dst_ref=target.at[b, me], send_sem=send_sem,
+                                         recv_sem=recv_sem.at[b], device_id=(to, kv), device_id_type=MESH).start()
+
+        def sends(i, _):
+            k = lax.div(i + 1, 2)
+            dz = Z // 2 + jnp.where(lax.rem(i, 2) == 1, -k, k)
+            for dy in dys:
+                for dc in range(2):
+                    send(dy, dz, dc)
+            return 0
+
+        lax.fori_loop(0, Z - 1, sends, 0)
+        for dy in dys:
+            for dc in range(2):
+                if (dy, dc) != (0, 0):
+                    send(dy, 0, dc)
+
+    def rest_of(b, source, send_sem, recv_sem):
+        rest = source.at[b, pl.ds(0, n - 1)]
+        return pltpu.make_async_remote_copy(src_ref=rest, dst_ref=rest, send_sem=send_sem, recv_sem=recv_sem.at[b],
+                                            device_id=(m.rank(0, 1, 0), kv), device_id_type=MESH)
+
+    for b in range(2):
+        to_all(b, far_first(Y), qpay, qrecv, qs, qrs)
     beside(len(order))
     wcopy.start()
-    g1.core_wait(Y * Z // 2, c1.at[0])
     wgive.start()
-    g3 = GatherZ(m, bufkv, pl.ds(0, 2 * kvr), both_cores, sems[3], sems[4], sems[5])
+    g3 = GatherZ(m, bufkv, pl.ds(0, 2 * kvr), both_cores, *sems[0:3])
     g3.start()
 
     nb = bp // CHUNK
 
     def rows_of(half):
-        return list(range(half * (Y // 2), (half + 1) * (Y // 2)))
-
-    def prepare(half):
-        for dy in rows_of(half):
-            yy = m.y_of(dy)
-
-            def widen(i, _):
-                f32s[pl.ds(pl.multiple_of((yy * (2 * Z) + i) * qr, qr), qr), :] = buf[yy, i].astype(F32)
-                return 0
-
-            lax.fori_loop(0, 2 * Z, widen, 0)
-        for b in range(2):
+        return far_first(Y)[half * (Y // 2):(half + 1) * (Y // 2)]
+
+    def prepare(b):
+        rest_of(b, qpay, qs, qrs).wait_recv()
+        f32s[0:n * 16, :] = qrecv[b].reshape(n * 16, 128).astype(F32)
+        for half in range(2):
             for s in range(MOST):
-                h = own_heads[b][s]
-                first = (h < per).astype(F32)
-                for t, dy in enumerate(rows_of(half)):
-                    qh = f32s[pl.ds(m.y_of(dy) * (row * heads) + h, row, stride=heads), :]
-                    qaug[2 * half + b, s * hp + t * row:s * hp + (t + 1) * row, :] = jnp.concatenate(
-                        [qh * first, qh * (1.0 - first)], axis=1).astype(BF16)
+                first = (own_heads[b][s] < per).astype(F32)
+                for i in range(rows):
+                    for t, dy in enumerate(rows_of(half)):
+                        qh = f32s[pl.ds(m.y_of(dy) * (2 * Z * 16) + s * rows + i, 2 * Z, stride=16), :]
+                        to = s * hp + (i * (Y // 2) + t) * (2 * Z)
+                        qaug[2 * b + half, to:to + 2 * Z, :] = jnp.concatenate(
+                            [qh * first, qh * (1.0 - first)], axis=1).astype(BF16)
 
     def both(even, odd, g):
-        at = pl.ds((g // nb % 2) * bp + g % nb * CHUNK, CHUNK)
+        at = pl.ds((g // nb // 2) * bp + g % nb * CHUNK, CHUNK)
         return jnp.concatenate([even[at, :], odd[at, :]], axis=1)
 
     def score(g):
@@ -298,9 +314,10 @@
             acc[u] = o
 
     def pack(unit):
-        u, b = unit % 2, unit % 2
+        u, b = unit % 2, unit // 2
+        places = hp // rows
         ln = lax.broadcasted_iota(jnp.int32, (hp, 128), 1)
-        rw = lax.rem(lax.broadcasted_iota(jnp.int32, (hp, 128), 0), rows)
+        rw = lax.div(lax.broadcasted_iota(jnp.int32, (hp, 128), 0), places)
         stat = jnp.zeros((hp, 128), F32)
         for s in range(MOST):
             sl = pl.ds(s * hp, hp)
@@ -314,46 +331,22 @@
             val = jnp.where(ln < 16, hi, jnp.where(ln < 32, mid, lo))
             stat = jnp.where((lax.rem(ln, 16) == s * rows + rw) & (ln < 48), val, stat)
         ob[MOST] = stat
-        for t, dy in enumerate(rows_of(unit // 2)):
-            for j in range(Z):
-                d = t * 2 * Z + 2 * j
-                for s in range(MOST + 1):
-                    x = ob[s, d * rows:(d + 2) * rows, :]
-                    pf[d * 16 + s * rows:d * 16 + (s + 1) * rows, :] = x[0:rows]
-                    pf[(d + 1) * 16 + s * rows:(d + 1) * 16 + (s + 1) * rows, :] = x[rows:2 * rows]
+        for s in range(MOST + 1):
+            for i in range(rows):
+                pf[pl.ds(s * rows + i, places, stride=16), :] = ob[s, i * places:(i + 1) * places, :]
+        for t, dy in enumerate(rows_of(unit % 2)):
             of_y = pf[t * 2 * Z * 16:(t + 1) * 2 * Z * 16, :].astype(BF16).reshape(2 * Z, 16, 128)
             pay[b, pl.ds(m.y_of(dy) * (2 * Z), 2 * Z)] = of_y
-        if unit // 2 == 0:
+        if 0 in rows_of(unit % 2):
             recv[b, me] = pay[b, me]
 
     def give(unit):
-        b = unit % 2
-        dys = rows_of(unit // 2)
-
-        def send(dy, dz, dc):
-            to = m.rank(dy, dz, dc)
-            pltpu.make_async_remote_copy(src_ref=pay.at[b, to], dst_ref=recv.at[b, me], send_sem=asend,
-                                         recv_sem=ar.at[b], device_id=(to, kv), device_id_type=MESH).start()
-
-        def sends(i, _):
-            k = lax.div(i + 1, 2)
-            dz = Z // 2 + jnp.where(lax.rem(i, 2) == 1, -k, k)
-            for dy in dys:
-                for dc in range(2):
-                    send(dy, dz, dc)
-            return 0
-
-        lax.fori_loop(0, Z - 1, sends, 0)
-        for dy in dys:
-            for dc in range(2):
-                if (dy, dc) != (0, 0):
-                    send(dy, 0, dc)
+        to_all(unit // 2, rows_of(unit % 2), pay, recv, asend, ar)
 
     prepare(0)
     score(0)
     for g in range(4 * nb + 1):
         if g + 1 == 2 * nb:
-            g1.core_wait(Y * Z // 2, c1.at[1])
             prepare(1)
         if g < 4 * nb:
             soften(g)
@@ -364,20 +357,16 @@
         if g >= 1 and g % nb == 0:
             pack(g // nb - 1)
             give(g // nb - 1)
-        if g == nb - 1:
-            for dz in [0] + near:
-                for dy in second_half:
-                    g1.along_y(dy, dz)
-                    g1.core(dy, dz, c1.at[1])
-        if g == 2 * nb:
+        if g == nb:
             g3.core(0, 0, c3)
             for dz in near:
                 g3.along_z(dz)
                 g3.core(0, dz, c3)
-    for dz in [0] + near:
-        for dy in range(1, Y):
-            g3.along_y(dy, dz)
-            g3.core(dy, dz, c3)
+        if g == 3 * nb:
+            for dz in [0] + near:
+                for dy in range(1, Y):
+                    g3.along_y(dy, dz)
+                    g3.core(dy, dz, c3)
     g3.core_wait(Y * Z, c3)
 
     def widenkv(i, _):
@@ -410,9 +399,7 @@
     own_l[...] = jnp.broadcast_to(om + jnp.log2(ot), (qr, 128))
 
     for b in range(2):
-        rest = pay.at[b, pl.ds(0, n - 1)]
-        pltpu.make_async_remote_copy(src_ref=rest, dst_ref=rest, send_sem=asend, recv_sem=ar.at[b],
-                                     device_id=(m.rank(0, 1, 0), kv), device_id_type=MESH).wait_recv()
+        rest_of(b, pay, asend, ar).wait_recv()
         f32s[b * n * 16:(b + 1) * n * 16, :] = recv[b].reshape(n * 16, 128).astype(F32)
     st = sum(f32s[pl.ds(MOST * rows + i, 2 * n, stride=16), :] for i in range(rows))
     st = (st + pltpu.roll(st, 128 - 16, 1)) + pltpu.roll(st, 128 - 32, 1)
@@ -443,8 +430,8 @@
         buf2[m.y, m.z, at, :] = a
 
     cut = qr - qr // 4
-    g2 = GatherZ(m, buf2, pl.ds(0, cut), one_core, *sems[6:9])
-    g4 = GatherY(m, buf2, pl.ds(cut, qr - cut), one_core, *sems[9:12])
+    g2 = GatherZ(m, buf2, pl.ds(0, cut), one_core, *sems[3:6])
+    g4 = GatherY(m, buf2, pl.ds(cut, qr - cut), one_core, *sems[6:9])
     g4.start()
     g2.start()
     for i, dz in enumerate(near):
@@ -483,14 +470,12 @@
                     pltpu.make_async_remote_copy(
                         src_ref=xp.at[k], dst_ref=part_ref.at[kv, m.c], send_sem=xs.at[k], recv_sem=xrs.at[k],
                         device_id=(m.rank(0, 0, dc), x), device_id_type=MESH).start()
-    g1.drain(True)
     g3.drain(True)
     g2.drain(False)
     g4.drain()
     for b in range(2):
-        rest = pay.at[b, pl.ds(0, n - 1)]
-        pltpu.make_async_remote_copy(src_ref=rest, dst_ref=rest, send_sem=asend, recv_sem=ar.at[b],
-                                     device_id=(m.rank(0, 1, 0), kv), device_id_type=MESH).wait_send()
+        rest_of(b, qpay, qs, qrs).wait_send()
+        rest_of(b, pay, asend, ar).wait_send()
     for dx in range(X):
         for dc in range(2):
             if (dx, dc) != (0, 0):
@@ -535,7 +520,7 @@
         vm((raw, width), BF16), vm((raw, width), BF16),
         vm((2 * bp, width), BF16), vm((2 * bp, width), BF16), vm((2 * bp, width), BF16), vm((2 * bp, width), BF16),
         vm((2, *out_weight.shape), BF16),
-        vm((Y, 2 * Z, qr, width), BF16), vm((Y, Z, qr, width), BF16), vm((Y, 2 * Z, 2 * kvr, width), BF16),
+        vm((2, n, 16, width), BF16), vm((2, n, 16, width), BF16), vm((Y, Z, qr, width), BF16), vm((Y, 2 * Z, 2 * kvr, width), BF16),
         vm((n * qr, width), F32), vm((n * 2 * kvr, width), F32), vm((part, width), F32),
         vm((4, unit, 2 * width), BF16),
         vm((2, unit, CHUNK), F32), vm((2, unit, width), F32), vm((2, unit, CHUNK), BF16), vm((2, unit, width), F32),
@@ -544,8 +529,8 @@
         vm((2, n, 16, width), BF16), vm((2, n, 16, width), BF16),
         vm((qr, width), F32), vm((qr, width), F32),
         vm((2 * X - 1, Z * rows, width), BF16),
-        dma((2 * (raw // part),)), dma, dma((2,)), dma, dma((2 * X - 1,)), dma((2 * X - 1,)), dma, dma, dma((2,)), dma,
-        *along_z, *along_z, *along_z, *along_y,
+        dma((2 * (raw // part),)), dma, dma((2,)), dma, dma((2 * X - 1,)), dma((2 * X - 1,)), dma, dma, dma, dma((2,)), dma,
+        *along_z, *along_z, *along_y,
     ]
     inv = pl.BlockSpec(memory_space=pltpu.VMEM)
     anyw = pl.BlockSpec(memory_space=pl.ANY)

time: 60.4 us -> 60.3 us (level)
  no operation moved by 1% of the time
where the time goes in v5:
time: 60.3 us; the launch traced here: 60.1 us
  Pallas kernels  59.4 us (99%)
  between operations  0.64 us (1%)
    pallas_call x1, Pallas kernels, local(): pl.pallas_call(kernel, out_shape=(jax.ShapeDtypeStruct((qr, width), BF16)...  58 us
    pallas_call x1, Pallas kernels, local(): pl.pallas_call(close, out_shape=(jax.ShapeDtypeStruct((qr, width), BF16),...  1.48 us

profile of v5, /device:TPU:1, one launch (start us, length us, event | category | flops | bytes accessed | tf_op | source)
XLA Modules:
  0.0 60.1 jit_solution(13145841140232268681)
XLA Ops:
  0.6 58.0 %sparse_attention.1 = (bf16[64,128]{1,0:T(8,128)(2,1)}, bf16[4,2,32,128]{3,2,1,0:T(8,128)(2,1)}) custom-call(bf16[64,128]{1,0:T(8,128)(2,1)} %bitcast.8, bf16[8,128]{1,0:T(8,128)(2,1)} %bitcast.9, bf16[8,128]{1,0:T(8,128)(2,1)} %bitcast.10, s32[16,12]{1,0:T(8,128)} %gat_ref.1, bf16[16384,128]{1,0:T(8,128)(2,1)} %bitcast.6, bf16[16384,128]{1,0:T(8,128)(2,1)} %bitcast.7, ...), custom_call_target="tpu_custom_call" | custom-call | tf_op jit(solution)/shard_map/sparse_attention/pallas_call | solution.py:537
  58.6 1.5 %close.1 = (bf16[64,128]{1,0:T(8,128)(2,1)}, bf16[64,128]{1,0:T(8,128)(2,1)}) custom-call(bf16[64,128]{1,0:T(8,128)(2,1)} %get-tuple-element.6.att_ref, bf16[4,2,32,128]{3,2,1,0:T(8,128)(2,1)} %get-tuple-element.7.part_ref), custom_call_target="tpu_custom_call" | custom-call | tf_op jit(solution)/shard_map/close/pallas_call | solution.py:549

commit v6 on v4

--- a/solution.py
+++ b/solution.py
@@ -10,7 +10,7 @@
 Y, Z, X = 4, 8, 4
 BLOCK_POSITIONS = 4096
 MOST = 3
-CHUNK = 2048
+CHUNK = 1024
 NEG = -1e30
 MESH = pl.DeviceIdType.MESH
 F32, BF16 = jnp.float32, jnp.bfloat16
@@ -243,20 +243,17 @@
     def prepare(half):
         for dy in rows_of(half):
             yy = m.y_of(dy)
-
-            def widen(i, _):
-                f32s[pl.ds(pl.multiple_of((yy * (2 * Z) + i) * qr, qr), qr), :] = buf[yy, i].astype(F32)
-                return 0
-
-            lax.fori_loop(0, 2 * Z, widen, 0)
+            f32s[pl.ds(yy * (2 * Z * qr), 2 * Z * qr), :] = buf[yy].reshape(2 * Z * qr, 128).astype(F32)
         for b in range(2):
             for s in range(MOST):
                 h = own_heads[b][s]
                 first = (h < per).astype(F32)
-                for t, dy in enumerate(rows_of(half)):
-                    qh = f32s[pl.ds(m.y_of(dy) * (row * heads) + h, row, stride=heads), :]
-                    qaug[2 * half + b, s * hp + t * row:s * hp + (t + 1) * row, :] = jnp.concatenate(
-                        [qh * first, qh * (1.0 - first)], axis=1).astype(BF16)
+                for i in range(rows):
+                    for t, dy in enumerate(rows_of(half)):
+                        qh = f32s[pl.ds(m.y_of(dy) * (row * heads) + i * heads + h, 2 * Z, stride=qr), :]
+                        to = s * hp + (i * (Y // 2) + t) * (2 * Z)
+                        qaug[2 * half + b, to:to + 2 * Z, :] = jnp.concatenate(
+                            [qh * first, qh * (1.0 - first)], axis=1).astype(BF16)
 
     def both(even, odd, g):
         at = pl.ds((g // nb % 2) * bp + g % nb * CHUNK, CHUNK)
@@ -299,8 +296,9 @@
 
     def pack(unit):
         u, b = unit % 2, unit % 2
+        places = hp // rows
         ln = lax.broadcasted_iota(jnp.int32, (hp, 128), 1)
-        rw = lax.rem(lax.broadcasted_iota(jnp.int32, (hp, 128), 0), rows)
+        rw = lax.div(lax.broadcasted_iota(jnp.int32, (hp, 128), 0), places)
         stat = jnp.zeros((hp, 128), F32)
         for s in range(MOST):
             sl = pl.ds(s * hp, hp)
@@ -314,13 +312,10 @@
             val = jnp.where(ln < 16, hi, jnp.where(ln < 32, mid, lo))
             stat = jnp.where((lax.rem(ln, 16) == s * rows + rw) & (ln < 48), val, stat)
         ob[MOST] = stat
+        for s in range(MOST + 1):
+            for i in range(rows):
+                pf[pl.ds(s * rows + i, places, stride=16), :] = ob[s, i * places:(i + 1) * places, :]
         for t, dy in enumerate(rows_of(unit // 2)):
-            for j in range(Z):
-                d = t * 2 * Z + 2 * j
-                for s in range(MOST + 1):
-                    x = ob[s, d * rows:(d + 2) * rows, :]
-                    pf[d * 16 + s * rows:d * 16 + (s + 1) * rows, :] = x[0:rows]
-                    pf[(d + 1) * 16 + s * rows:(d + 1) * 16 + (s + 1) * rows, :] = x[rows:2 * rows]
             of_y = pf[t * 2 * Z * 16:(t + 1) * 2 * Z * 16, :].astype(BF16).reshape(2 * Z, 16, 128)
             pay[b, pl.ds(m.y_of(dy) * (2 * Z), 2 * Z)] = of_y
         if unit // 2 == 0:
@@ -380,12 +375,7 @@
             g3.core(dy, dz, c3)
     g3.core_wait(Y * Z, c3)
 
-    def widenkv(i, _):
-        kv32[pl.ds(pl.multiple_of(i * 2 * kvr, 2 * kvr), 2 * kvr), :] = (
-            bufkv[lax.div(i, 2 * Z), lax.rem(i, 2 * Z)].astype(F32))
-        return 0
-
-    lax.fori_loop(0, n, widenkv, 0)
+    kv32[...] = bufkv[...].reshape(n * 2 * kvr, 128).astype(F32)
     kk, vvv = [], []
     for g in range(2):
         kk.append(jnp.concatenate([kv32[pl.ds(2 * i + g, n, stride=2 * kvr), :] for i in range(rows)], axis=0))

time: 60.4 us -> 58.7 us (0.972)
  Pallas kernels: 59.5 us -> 57.9 us
    pallas_call x1, Pallas kernels: 58.1 us -> 56.4 us  [local(): pl.pallas_call(kernel, out_shape=(jax.ShapeDtypeStruct((qr, width), BF16)...]
where the time goes in v6:
time: 58.7 us; the launch traced here: 58.5 us
  Pallas kernels  57.9 us (99%)
  between operations  0.64 us (1%)
    pallas_call x1, Pallas kernels, local(): pl.pallas_call(kernel, out_shape=(jax.ShapeDtypeStruct((qr, width), BF16)...  56.4 us
    pallas_call x1, Pallas kernels, local(): pl.pallas_call(close, out_shape=(jax.ShapeDtypeStruct((qr, width), BF16),...  1.48 us

profile of v6, /device:TPU:1, one launch (start us, length us, event | category | flops | bytes accessed | tf_op | source)
XLA Modules:
  0.0 58.5 jit_solution(8503188256807930424)
XLA Ops:
  0.6 56.4 %sparse_attention.1 = (bf16[64,128]{1,0:T(8,128)(2,1)}, bf16[4,2,32,128]{3,2,1,0:T(8,128)(2,1)}) custom-call(bf16[64,128]{1,0:T(8,128)(2,1)} %bitcast.8, bf16[8,128]{1,0:T(8,128)(2,1)} %bitcast.9, bf16[8,128]{1,0:T(8,128)(2,1)} %bitcast.10, s32[16,12]{1,0:T(8,128)} %gat_ref.1, bf16[16384,128]{1,0:T(8,128)(2,1)} %bitcast.6, bf16[16384,128]{1,0:T(8,128)(2,1)} %bitcast.7, ...), custom_call_target="tpu_custom_call" | custom-call | tf_op jit(solution)/shard_map/sparse_attention/pallas_call | solution.py:542
  57.0 1.5 %close.1 = (bf16[64,128]{1,0:T(8,128)(2,1)}, bf16[64,128]{1,0:T(8,128)(2,1)}) custom-call(bf16[64,128]{1,0:T(8,128)(2,1)} %get-tuple-element.6.att_ref, bf16[4,2,32,128]{3,2,1,0:T(8,128)(2,1)} %get-tuple-element.7.part_ref), custom_call_target="tpu_custom_call" | custom-call | tf_op jit(solution)/shard_map/close/pallas_call | solution.py:554

commit v7 on v6

--- a/solution.py
+++ b/solution.py
@@ -164,6 +164,41 @@
                 pl.semaphore_signal(bar, inc=1, device_id=(m.rank(0, 0, dc), lax.rem(kv + dx, X)), device_id_type=MESH)
     buf[m.y, zc] = q_ref[...]
     bufkv[m.y, zc] = jnp.concatenate([sk_ref[...], sv_ref[...]], axis=0)
+
+    part = d32.shape[0]
+    parts = kraw.shape[0] // part
+    order = [(a, blk * (parts // 2) + i) for blk in range(2) for a in range(2) for i in range(parts // 2)]
+    arrays = ((kc_ref, kraw, k0, k1), (vc_ref, vraw, v0, v1))
+
+    def load(j):
+        a, i = order[j]
+        at = pl.ds(i * part, part)
+        return pltpu.make_async_copy(arrays[a][0].at[at], arrays[a][1].at[at], loc.at[j])
+
+    def pieces():
+        for j, (a, i) in enumerate(order):
+            load(j).wait()
+            _, raw, even, odd = arrays[a]
+            to = pl.ds(i * (part // 2), part // 2)
+            d32[...] = raw[pl.ds(i * part, part), :].astype(F32)
+            even[to, :] = d32[pl.ds(0, part // 2, stride=2), :].astype(BF16)
+            odd[to, :] = d32[pl.ds(1, part // 2, stride=2), :].astype(BF16)
+            yield
+
+    work = pieces()
+
+    def beside(number):
+        for _ in range(number):
+            next(work, None)
+
+    for j in range(len(order)):
+        load(j).start()
+    pl.semaphore_wait(bar, Z - 1 + Y - 1 + 2 * X - 1)
+
+    near = near_first(Z)
+    g1 = GatherZ(m, buf, pl.ds(0, qr), both_cores, sems[0], sems[1], sems[2], ahead=range(Y - 1, 0, -1))
+    g1.start()
+    g1.core(0, 0, c1.at[0])
 
     lane = lax.broadcasted_iota(jnp.int32, (heads, 2 * n), 1)
     block_of = lax.rem(lane, n) * 2 + lax.div(lane, n)
@@ -182,41 +217,6 @@
     own_heads = [[jnp.maximum(jnp.max(jnp.where(lane1 == b * n + me, hm[s], -1)), 0) for s in range(MOST)]
                  for b in range(2)]
 
-    part = d32.shape[0]
-    parts = kraw.shape[0] // part
-    order = [(a, blk * (parts // 2) + i) for blk in range(2) for a in range(2) for i in range(parts // 2)]
-    arrays = ((kc_ref, kraw, k0, k1), (vc_ref, vraw, v0, v1))
-
-    def load(j):
-        a, i = order[j]
-        at = pl.ds(i * part, part)
-        return pltpu.make_async_copy(arrays[a][0].at[at], arrays[a][1].at[at], loc.at[j])
-
-    def pieces():
-        for j, (a, i) in enumerate(order):
-            load(j).wait()
-            _, raw, even, odd = arrays[a]
-            to = pl.ds(i * (part // 2), part // 2)
-            d32[...] = raw[pl.ds(i * part, part), :].astype(F32)
-            even[to, :] = d32[pl.ds(0, part // 2, stride=2), :].astype(BF16)
-            odd[to, :] = d32[pl.ds(1, part // 2, stride=2), :].astype(BF16)
-            yield
-
-    work = pieces()
-
-    def beside(number):
-        for _ in range(number):
-            next(work, None)
-
-    for j in range(len(order)):
-        load(j).start()
-    beside(2)
-    pl.semaphore_wait(bar, Z - 1 + Y - 1 + 2 * X - 1)
-
-    near = near_first(Z)
-    g1 = GatherZ(m, buf, pl.ds(0, qr), both_cores, sems[0], sems[1], sems[2], ahead=range(Y - 1, 0, -1))
-    g1.start()
-    g1.core(0, 0, c1.at[0])
     beside(len(order) * 3 // 8)
     for dz in near:
         g1.along_z(dz)

time: 58.7 us -> 58.8 us (level)
  no operation moved by 1% of the time
where the time goes in v7:
time: 58.8 us; the launch traced here: 58.5 us
  Pallas kernels  57.9 us (98%)
  between operations  0.64 us (1%)
    pallas_call x1, Pallas kernels, local(): pl.pallas_call(kernel, out_shape=(jax.ShapeDtypeStruct((qr, width), BF16)...  56.4 us
    pallas_call x1, Pallas kernels, local(): pl.pallas_call(close, out_shape=(jax.ShapeDtypeStruct((qr, width), BF16),...  1.48 us

profile of v7, /device:TPU:1, one launch (start us, length us, event | category | flops | bytes accessed | tf_op | source)
XLA Modules:
  0.0 58.5 jit_solution(9280709815403634997)
XLA Ops:
  0.6 56.4 %sparse_attention.1 = (bf16[64,128]{1,0:T(8,128)(2,1)}, bf16[4,2,32,128]{3,2,1,0:T(8,128)(2,1)}) custom-call(bf16[64,128]{1,0:T(8,128)(2,1)} %bitcast.8, bf16[8,128]{1,0:T(8,128)(2,1)} %bitcast.9, bf16[8,128]{1,0:T(8,128)(2,1)} %bitcast.10, s32[16,12]{1,0:T(8,128)} %gat_ref.1, bf16[16384,128]{1,0:T(8,128)(2,1)} %bitcast.6, bf16[16384,128]{1,0:T(8,128)(2,1)} %bitcast.7, ...), custom_call_target="tpu_custom_call" | custom-call | tf_op jit(solution)/shard_map/sparse_attention/pallas_call | solution.py:542
  57.0 1.5 %close.1 = (bf16[64,128]{1,0:T(8,128)(2,1)}, bf16[64,128]{1,0:T(8,128)(2,1)}) custom-call(bf16[64,128]{1,0:T(8,128)(2,1)} %get-tuple-element.6.att_ref, bf16[4,2,32,128]{3,2,1,0:T(8,128)(2,1)} %get-tuple-element.7.part_ref), custom_call_target="tpu_custom_call" | custom-call | tf_op jit(solution)/shard_map/close/pallas_call | solution.py:554
